TPU v7x, 128 devices: a whole 4x4x4 slice. The times are simulated.
128 devices in a mesh: tile: 64 (over y, z, x), chan: 2 (over core).
Axes of the slice: x: 4, y: 4, z: 4, core: 2. Of those that a mesh axis runs over, the one named last changes fastest.
Arguments:
- attributes: bfloat16 [35, 1024, 512], P(None, 'tile'), may hold values from -6 to 6
- cell_basin: int32 [1024, 512], P('tile'), may hold values from 0 to 8191, as said below
- basin_cells: int32 [8192], P('tile'), may hold values from 1 to 127, as said below
- conv_first: bfloat16 [128, 3, 3, 35], P('chan'), may hold values from -0.5 to 0.5
- conv_second: bfloat16 [128, 3, 3, 128], P('chan'), may hold values from -0.25 to 0.25
- conv_third: bfloat16 [128, 3, 3, 128], P('chan'), may hold values from -0.25 to 0.25
- head_weight: bfloat16 [128, 12], P('chan'), may hold values from -0.75 to 0.75
- precip: float32 [30, 16, 8192], P(None, 'chan', 'tile'), may hold values from 0 to 250
- temp: float32 [30, 16, 8192], P(None, 'chan', 'tile'), may hold values from -24 to 24
- pet: float32 [30, 16, 8192], P(None, 'chan', 'tile'), may hold values from 0.5 to 4
Outputs:
- streamflow: float32 [30, 16, 8192], P(None, 'chan', 'tile')
Inputs may be any that keep to these rules, and one draw needn't show every extreme that they name: `cell_basin`: in each tile the 8192 cells in row-major order form 64 runs of 128 cells; the runs of one tile go to 64 different owners, so that every owner receives exactly 128 cells from every tile. The basins of owner o are o * 128 to o * 128 + 127; one run holds 2 whole basins, each a contiguous part of the run. `basin_cells`: the number of cells of cell_basin in each basin; some basin reaches the most.
All inputs are finite; a program needn't handle non-finite values.
Results may differ from a plain program's by a relative error of at most 0.00061.
Values may be sent and summed in bfloat16 or wider, within the bound.
A program may use at most 64 MiB of HBM per device.

v0:
```python
import jax
import jax.numpy as jnp
from jax import lax
from jax.sharding import PartitionSpec as P

LAGS = 15


LOW = [-2.0, 0.5, 50.0, 1.0, 0.3, 0.05, 0.01, 0.001, 0.0, 0.5, 1.0, 0.5]
SPAN = [4.0, 5.5, 450.0, 4.0, 0.7, 0.45, 0.29, 0.099, 50.0, 5.5, 2.0, 2.5]


def padded_2(cells, sides, width):
    for axis, dim in sides:
        count = lax.axis_size(axis)
        ends = count - 1
        head = lax.slice_in_dim(cells, 0, width, axis=dim)
        tail = lax.slice_in_dim(cells, cells.shape[dim] - width, cells.shape[dim], axis=dim)
        cells = jnp.concatenate(
            [
                lax.ppermute(tail, axis, [(i, (i + 1) % count) for i in range(ends)]),
                cells,
                lax.ppermute(head, axis, [((i + 1) % count, i) for i in range(ends)]),
            ],
            axis=dim,
        )
    return cells


def pad_columns(field):
    return jnp.pad(field, ((0, 0), (0, 0), (1, 1)))


def conv_taps(total, weight, padded):
    height = total.shape[1]
    width = total.shape[2]
    for row_tap in range(3):
        for col_tap in range(3):
            taps = weight[:, row_tap, col_tap, :]
            window = padded[:, row_tap : row_tap + height, col_tap : col_tap + width]
            total = total + jnp.einsum(
                "oc,chw->ohw", taps, window, preferred_element_type=jnp.float32
            )
    return total


def bucket_run(param, precip, temp, pet):
    tt, cfmax, fc, beta, lp = (param[0], param[1], param[2], param[3], param[4])
    k0, k1, k2, uzl, perc = (param[5], param[6], param[7], param[8], param[9])

    def day(state, force):
        snow, soil, upper, lower = state
        rain_in, air, demand = force
        liquid = jax.nn.sigmoid(air - tt)
        gained = snow + rain_in * (1.0 - liquid)
        snow_new = jnp.maximum(gained - cfmax * jnp.maximum(air - tt, 0.0), 0.0)
        melt = gained - snow_new
        inflow = rain_in * liquid + melt
        recharge = inflow * jnp.power(soil / fc, beta)
        soil = soil + inflow - recharge
        excess = jnp.maximum(soil - fc, 0.0)
        soil = soil - excess
        soil = jnp.where(soil < lp * fc, soil * (1.0 - demand / (lp * fc)), soil - demand)
        upper = upper + recharge + excess
        upper_new = jnp.maximum(upper - perc, 0.0)
        lower = lower + upper - upper_new
        quick = k0 * jnp.maximum(upper_new - uzl, 0.0)
        slow = k1 * upper_new
        upper = upper_new - quick - slow
        base = k2 * lower
        lower = lower - base
        return ((snow_new, soil, upper, lower), quick + slow + base)

    shape = precip.shape[1:]
    start = (
        jnp.zeros(shape, jnp.float32),
        jnp.broadcast_to(0.5 * fc, shape),
        jnp.full(shape, 5.0, jnp.float32),
        jnp.full(shape, 20.0, jnp.float32),
    )
    final, runoff = lax.scan(day, start, (precip, temp, pet))
    return runoff


def route(param, runoff):
    days = runoff.shape[0]
    lag = jnp.arange(LAGS).astype(jnp.float32) + 0.5
    weight = jnp.exp(
        (param[10] - 1.0)[None, :] * jnp.log(lag)[:, None] - lag[:, None] / param[11][None, :]
    )
    weight = weight / jnp.sum(weight, axis=0, keepdims=True)
    later = jnp.arange(days)[:, None] - jnp.arange(days)[None, :]
    pick = (later[None, :, :] == jnp.arange(LAGS)[:, None, None]).astype(jnp.float32)
    matrix = jnp.einsum("kts,kb->tsb", pick, weight, precision=lax.Precision.HIGHEST)
    return jnp.einsum("tsb,swb->twb", matrix, runoff, precision=lax.Precision.HIGHEST)


def on_device(
    attributes,
    cell_basin,
    basin_cells,
    conv_first,
    conv_second,
    conv_third,
    head_weight,
    precip,
    temp,
    pet,
):
    height = attributes.shape[1]
    width = attributes.shape[2]
    n_chan = lax.axis_size("chan")
    owners = lax.axis_size("tile")
    half = height // n_chan
    rimmed = padded_2(attributes, (("tile", 1),), 1)
    empty = jnp.zeros((conv_first.shape[0], height, width), jnp.float32)
    first = conv_taps(empty, conv_first, pad_columns(rimmed))
    hidden = jnp.maximum(first, 0.0).astype(jnp.bfloat16)
    for weight in (conv_second, conv_third):
        rim = padded_2(hidden, (("tile", 1),), 1)
        total = conv_taps(
            empty, weight, pad_columns(lax.all_gather(rim, "chan", axis=0, tiled=True))
        )
        hidden = jnp.maximum(total, 0.0).astype(jnp.bfloat16)
    raw = lax.psum_scatter(
        jnp.einsum("cp,chw->hpw", head_weight, hidden, preferred_element_type=jnp.float32),
        "chan",
        scatter_dimension=0,
        tiled=True,
    )
    params_count = raw.shape[1]
    share = jnp.transpose(jax.nn.sigmoid(raw), (1, 0, 2)).reshape(params_count, -1)
    mine = lax.dynamic_slice_in_dim(cell_basin, lax.axis_index("chan") * half, half, 0).reshape(-1)
    basins_here = basin_cells.shape[0]
    sums = jax.ops.segment_sum(share.T, mine, num_segments=owners * basins_here)
    sums = sums.T.reshape(params_count, owners, basins_here)
    arrived = lax.all_to_all(sums, "tile", split_axis=1, concat_axis=1, tiled=True)
    partial_value = jnp.sum(arrived, axis=1)
    total_sum = lax.psum(partial_value, "chan")
    mean = total_sum / basin_cells.astype(jnp.float32)[None, :]
    param = jnp.array(LOW, jnp.float32)[:, None] + jnp.array(SPAN, jnp.float32)[:, None] * mean
    runoff = bucket_run(param, precip, temp, pet)
    return route(param, runoff)


def solution(mesh):
    return jax.shard_map(
        on_device,
        mesh=mesh,
        in_specs=(
            P(None, "tile", None),
            P("tile", None),
            P("tile"),
            P("chan", None, None, None),
            P("chan", None, None, None),
            P("chan", None, None, None),
            P("chan", None),
            P(None, "chan", "tile"),
            P(None, "chan", "tile"),
            P(None, "chan", "tile"),
        ),
        out_specs=P(None, "chan", "tile"),
        check_vma=False,
    )
```

profile of v0, /device:TPU:1, one launch (start us, length us, event | category | flops | bytes accessed | tf_op | source)
XLA Modules:
  0.0 255.4 jit_solution(3265855978443713015)
XLA Ops:
  6.5 1.4 copy.77
  7.9 3.9 %collective-permute-start = (bf16[35,1,512]{2,0,1:T(8,128)(2,1)S(1)}, bf16[35,1,512]{2,0,1:T(8,128)(2,1)S(1)}, u32[]{:S(2)}, u32[]{:S(2)}) collective-permute-start(bf16[35,1,512]{2,0,1:T(8,128)(2,1)S(1)} %get-tuple-element.376), channel_id=1, source_target_pairs={{0,2},{2,4},{4,6},{6,8},{8,10},{10,12},{12,14},{14,16},{16,18},{18... | collective-permute-start | bytes 107528 | tf_op jit(solution)/shard_map/ppermute | solution.py:21
  11.9 1.4 collective-permute-start.1
  13.3 1.7 fusion.113
  15.1 1.7 collective-permute-done.1
  20.9 2.4 fusion.36
  23.3 3.2 %collective-permute-start.2 = (bf16[64,1,512]{2,0,1:T(8,128)(2,1)S(1)}, bf16[64,1,512]{2,0,1:T(8,128)(2,1)S(1)}, u32[]{:S(2)}, u32[]{:S(2)}) collective-permute-start(bf16[64,1,512]{2,0,1:T(8,128)(2,1)S(1)} %get-tuple-element.374), channel_id=1, source_target_pairs={{0,2},{2,4},{4,6},{6,8},{8,10},{10,12},{12,14},{14,16},{16,18},{18... | collective-permute-start | bytes 196616 | tf_op jit(solution)/shard_map/ppermute | solution.py:21
  27.9 3.7 %collective-permute-done.3 = bf16[64,1,512]{2,0,1:T(8,128)(2,1)S(1)} collective-permute-done((bf16[64,1,512]{2,0,1:T(8,128)(2,1)S(1)}, bf16[64,1,512]{2,0,1:T(8,128)(2,1)S(1)}, u32[]{:S(2)}, u32[]{:S(2)}) %collective-permute-start.3) | collective-permute-done | bytes 65568 | tf_op jit(solution)/shard_map/ppermute | solution.py:23
  33.0 24.5 %all-gather.3.cloned.1.call-done = bf16[128,18,512]{2,0,1:T(8,128)(2,1)} async-done(((bf16[64,18,512]{2,0,1:T(8,128)(2,1)}), bf16[128,18,512]{2,0,1:T(8,128)(2,1)}) %all-gather.3.cloned.1.call-update) | async-done | bytes 2359312 | tf_op jit(solution)/shard_map/all_gather | solution.py:122
  57.5 2.5 fusion.11
  64.5 1.5 fusion.40
  66.1 3.3 %collective-permute-start.4 = (bf16[64,1,512]{2,0,1:T(8,128)(2,1)S(1)}, bf16[64,1,512]{2,0,1:T(8,128)(2,1)S(1)}, u32[]{:S(2)}, u32[]{:S(2)}) collective-permute-start(bf16[64,1,512]{2,0,1:T(8,128)(2,1)S(1)} %get-tuple-element.372), channel_id=1, source_target_pairs={{0,2},{2,4},{4,6},{6,8},{8,10},{10,12},{12,14},{14,16},{16,18},{18... | collective-permute-start | bytes 196616 | tf_op jit(solution)/shard_map/ppermute | solution.py:21
  70.7 3.7 %collective-permute-done.5 = bf16[64,1,512]{2,0,1:T(8,128)(2,1)S(1)} collective-permute-done((bf16[64,1,512]{2,0,1:T(8,128)(2,1)S(1)}, bf16[64,1,512]{2,0,1:T(8,128)(2,1)S(1)}, u32[]{:S(2)}, u32[]{:S(2)}) %collective-permute-start.5) | collective-permute-done | bytes 65568 | tf_op jit(solution)/shard_map/ppermute | solution.py:23
  75.9 19.4 %all-gather.5.cloned.1.call-done = bf16[128,18,512]{2,0,1:T(8,128)(2,1)} async-done(((bf16[64,18,512]{2,0,1:T(8,128)(2,1)}), bf16[128,18,512]{2,0,1:T(8,128)(2,1)}) %all-gather.5.cloned.1.call-update) | async-done | bytes 2359312 | tf_op jit(solution)/shard_map/all_gather | solution.py:122
  95.3 3.9 %fusion.17 = f32[16,512,64]{1,2,0:T(8,128)} fusion(bf16[128,18,512]{2,0,1:T(8,128)(2,1)} %all-gather.5.cloned.1.call-done, bf16[64,3,3,128]{3,0,2,1:T(8,128)(2,1)S(1)} %copy-done.3), kind=kOutput, calls=%fused_computation.49 | convolution fusion | flops 134217728 | bytes 4472832 | tf_op jit(solution)/shard_map/oc,chw->ohw/dot_general | solution.py:41
  99.2 2.1 fusion.18
  101.3 2.2 fusion.19
  103.4 2.2 fusion.20
  105.6 2.1 fusion.21
  107.8 1.8 fusion.23
  109.5 1.7 fusion.25
  111.3 1.7 fusion.27
  113.0 8.3 %fusion.43 = f32[16,12,512]{2,1,0:T(8,128)} fusion(bf16[128,18,512]{2,0,1:T(8,128)(2,1)S(1)} %copy-done.1, f32[16,512,64]{1,2,0:T(8,128)} %fusion.23, f32[16,512,64]{1,2,0:T(8,128)} %fusion.21, f32[16,512,64]{1,2,0:T(8,128)} %fusion.20, f32[16,512,64]{1,2,0:T(8,128)} %fusion.25, f32[16,512,64]{1,2,0:T(8,128)} %fusion.19, f32[16,512,64]{1,2,0:T(8,128)} %fusion.18, ...), kind=kOutput, calls=%fused_computation.83 | convolution fusion | flops 152043520 | bytes 19550208 | tf_op jit(solution)/shard_map/cp,chw->hpw/dot_general | solution.py:126
  121.4 12.1 %reduce-scatter.2.cloned.1.call-done = f32[8,12,512]{2,1,0:T(8,128)} async-done(((f32[16,12,512]{2,1,0:T(8,128)}), f32[8,12,512]{2,1,0:T(8,128)}) %reduce-scatter.2.cloned.1.call-update) | async-done | bytes 196624 | tf_op jit(solution)/shard_map/reduce_scatter | solution.py:125
  135.4 30.7 %scatter_custom_fusion = f32[8192,12]{1,0:T(8,128)} fusion(s32[4096]{0:T(1024)S(1)} %bitcast.289, f32[4096,12]{1,0:T(8,128)S(1)} %copy.84, f32[]{:T(128)} %constant.50.clone.1), kind=kCustom, calls=%fused_computation.76 | custom fusion | flops 49152 | bytes 393220 | tf_op jit(solution)/shard_map/scatter-add | solution.py:135
  166.2 3.6 %copy.85 = f32[12,64,128]{2,0,1:T(8,128)} copy(f32[12,64,128]{0,2,1:T(8,128)} %bitcast.269) | data formatting | bytes 786432 | tf_op jit(solution)/shard_map/reshape | solution.py:136
  169.8 10.1 %all-to-all-start = ((f32[12,64,128]{2,0,1:T(8,128)}), f32[12,64,128]{2,0,1:T(8,128)S(1)}, u32[]{:S(2)}, u32[]{:S(2)}) async-start(f32[12,64,128]{2,0,1:T(8,128)} %copy.85), calls=%async_computation.1 | async-start | bytes 1048576 | tf_op jit(solution)/shard_map/all_to_all | solution.py:137
  180.0 12.6 %all-to-all-done = f32[12,64,128]{2,0,1:T(8,128)S(1)} async-done(((f32[12,64,128]{2,0,1:T(8,128)}), f32[12,64,128]{2,0,1:T(8,128)S(1)}, u32[]{:S(2)}, u32[]{:S(2)}) %all-to-all-start) | async-done | bytes 393248 | tf_op jit(solution)/shard_map/all_to_all | solution.py:137
  192.7 3.8 %psum.7 = f32[12,128]{1,0:T(8,128)S(1)} all-reduce(f32[12,128]{1,0:T(8,128)S(1)} %reduce_sum.18), channel_id=1, replica_groups=mesh['tile'=64,'chan'=2] {'chan'}, use_global_device_ids=true, to_apply=%region_3.4 | all-reduce | flops 1536 | bytes 12288 | tf_op jit(solution)/shard_map/psum | solution.py:139
  197.4 1.9 copy.89
  199.3 45.1 %while.21 = (s32[]{:T(128)}, f32[8,128]{1,0:T(8,128)S(1)}, f32[8,128]{1,0:T(8,128)S(1)}, f32[8,128]{1,0:T(8,128)S(1)}, f32[8,128]{1,0:T(8,128)S(1)}, /*index=5*/...) while((s32[]{:T(128)}, f32[8,128]{1,0:T(8,128)S(1)}, ...), condition=%wide.region_5.6_spmd.clone, body=%wide.region_4.5_spmd.clone.sunk | while | flops 63491 | bytes 82640 | solution.py:81
  244.6 3.4 %convolution_bitcast_fusion = f32[30,8,128]{0,1,2:T(8,128)S(1)} fusion(f32[30,8,128]{0,1,2:T(8,128)S(1)} %copy.88, f32[30,30,128]{1,0,2:T(8,128)S(1)} %copy.89), kind=kOutput, calls=%fused_computation.82 | convolution fusion | flops 11059200 | bytes 706560 | tf_op jit(solution)/shard_map/tsb,swb->twb/dot_general | solution.py:95
  (134 shorter events, 62.4 us)
Async XLA Ops:
  6.5 114.8 %copy-start = (s32[16,512]{1,0:T(8,128)S(1)}, s32[16,512]{1,0:T(8,128)}, u32[]{:S(2)}) copy-start(s32[16,512]{1,0:T(8,128)} %param.15) | copy-start | bytes 98308
  6.5 51.0 %all-gather.3.cloned.1.call-start = ((), (), s32[]{:S(2)}) async-start(), calls=%async_computation.2 | async-start | bytes 3538944 | tf_op jit(solution)/shard_map/all_gather | solution.py:122
  7.9 7.1 %collective-permute-start = (bf16[35,1,512]{2,0,1:T(8,128)(2,1)S(1)}, bf16[35,1,512]{2,0,1:T(8,128)(2,1)S(1)}, u32[]{:S(2)}, u32[]{:S(2)}) collective-permute-start(bf16[35,1,512]{2,0,1:T(8,128)(2,1)S(1)} %get-tuple-element.376), channel_id=1, source_target_pairs={{0,2},{2,4},{4,6},{6,8},{8,10},{10,12},{12,14},{14,16},{16,18},{18... | collective-permute-start | bytes 107528 | tf_op jit(solution)/shard_map/ppermute | solution.py:21
  11.9 5.4 %copy-start.5 = (bf16[64,3,3,35]{0,3,2,1:T(8,128)(2,1)S(1)}, bf16[64,3,3,35]{0,3,2,1:T(8,128)(2,1)}, u32[]{:S(2)}) copy-start(bf16[64,3,3,35]{0,3,2,1:T(8,128)(2,1)} %param.17) | copy-start | bytes 120964
  11.9 4.9 %collective-permute-start.1 = (bf16[35,1,512]{2,0,1:T(8,128)(2,1)S(1)}, bf16[35,1,512]{2,0,1:T(8,128)(2,1)S(1)}, u32[]{:S(2)}, u32[]{:S(2)}) collective-permute-start(bf16[35,1,512]{2,0,1:T(8,128)(2,1)S(1)} %get-tuple-element.377), channel_id=1, source_target_pairs={{2,0},{4,2},{6,4},{8,6},{10,8},{12,10},{14,12},{16,14},{18,16},{20... | collective-permute-start | bytes 107528 | tf_op jit(solution)/shard_map/ppermute | solution.py:23
  23.3 34.2 %copy-start.4 = (bf16[64,3,3,128]{3,0,2,1:T(8,128)(2,1)S(1)}, bf16[64,3,3,128]{3,0,2,1:T(8,128)(2,1)}, u32[]{:S(2)}) copy-start(bf16[64,3,3,128]{3,0,2,1:T(8,128)(2,1)} %param.18) | copy-start | bytes 442372
  23.3 4.6 %collective-permute-start.2 = (bf16[64,1,512]{2,0,1:T(8,128)(2,1)S(1)}, bf16[64,1,512]{2,0,1:T(8,128)(2,1)S(1)}, u32[]{:S(2)}, u32[]{:S(2)}) collective-permute-start(bf16[64,1,512]{2,0,1:T(8,128)(2,1)S(1)} %get-tuple-element.374), channel_id=1, source_target_pairs={{0,2},{2,4},{4,6},{6,8},{8,10},{10,12},{12,14},{14,16},{16,18},{18... | collective-permute-start | bytes 196616 | tf_op jit(solution)/shard_map/ppermute | solution.py:21
  26.6 5.0 %collective-permute-start.3 = (bf16[64,1,512]{2,0,1:T(8,128)(2,1)S(1)}, bf16[64,1,512]{2,0,1:T(8,128)(2,1)S(1)}, u32[]{:S(2)}, u32[]{:S(2)}) collective-permute-start(bf16[64,1,512]{2,0,1:T(8,128)(2,1)S(1)} %get-tuple-element.375), channel_id=1, source_target_pairs={{2,0},{4,2},{6,4},{8,6},{10,8},{12,10},{14,12},{16,14},{18,16},{20... | collective-permute-start | bytes 196616 | tf_op jit(solution)/shard_map/ppermute | solution.py:23
  32.8 62.5 %all-gather.5.cloned.1.call-start = ((), (), s32[]{:S(2)}) async-start(), calls=%async_computation.3 | async-start | bytes 3538944 | tf_op jit(solution)/shard_map/all_gather | solution.py:122
  57.5 2.5 copy-start.2
  66.0 29.3 %copy-start.3 = (bf16[64,3,3,128]{3,0,2,1:T(8,128)(2,1)S(1)}, bf16[64,3,3,128]{3,0,2,1:T(8,128)(2,1)}, u32[]{:S(2)}) copy-start(bf16[64,3,3,128]{3,0,2,1:T(8,128)(2,1)} %param.19) | copy-start | bytes 442372
  66.1 4.6 %collective-permute-start.4 = (bf16[64,1,512]{2,0,1:T(8,128)(2,1)S(1)}, bf16[64,1,512]{2,0,1:T(8,128)(2,1)S(1)}, u32[]{:S(2)}, u32[]{:S(2)}) collective-permute-start(bf16[64,1,512]{2,0,1:T(8,128)(2,1)S(1)} %get-tuple-element.372), channel_id=1, source_target_pairs={{0,2},{2,4},{4,6},{6,8},{8,10},{10,12},{12,14},{14,16},{16,18},{18... | collective-permute-start | bytes 196616 | tf_op jit(solution)/shard_map/ppermute | solution.py:21
  69.4 5.0 %collective-permute-start.5 = (bf16[64,1,512]{2,0,1:T(8,128)(2,1)S(1)}, bf16[64,1,512]{2,0,1:T(8,128)(2,1)S(1)}, u32[]{:S(2)}, u32[]{:S(2)}) collective-permute-start(bf16[64,1,512]{2,0,1:T(8,128)(2,1)S(1)} %get-tuple-element.373), channel_id=1, source_target_pairs={{2,0},{4,2},{6,4},{8,6},{10,8},{12,10},{14,12},{16,14},{18,16},{20... | collective-permute-start | bytes 196616 | tf_op jit(solution)/shard_map/ppermute | solution.py:23
  75.6 57.8 %reduce-scatter.2.cloned.1.call-start = ((), (), s32[]{:S(2)}) async-start(), calls=%async_computation.4 | async-start | bytes 786432 | tf_op jit(solution)/shard_map/reduce_scatter | solution.py:125
  95.3 3.9 %copy-start.1 = (bf16[128,18,512]{2,0,1:T(8,128)(2,1)S(1)}, bf16[128,18,512]{2,0,1:T(8,128)(2,1)}, u32[]{:S(2)}) copy-start(bf16[128,18,512]{2,0,1:T(8,128)(2,1)} %all-gather.5.cloned.1.call-done) | copy-start | bytes 7077892
  111.3 1.7 copy-start.6
  166.2 13.8 %copy-start.9 = (s32[128]{0:T(128)S(1)}, s32[128]{0:T(128)}, u32[]{:S(2)}) copy-start(s32[128]{0:T(128)} %param.16) | copy-start | bytes 1540
  166.2 30.4 %copy-start.7 = (f32[12]{0:T(128)S(1)}, f32[12]{0:T(128)}, u32[]{:S(2)}) copy-start(f32[12]{0:T(128)} %constant.60.clone) | copy-start | bytes 148
  166.2 30.4 %copy-start.8 = (f32[12]{0:T(128)S(1)}, f32[12]{0:T(128)}, u32[]{:S(2)}) copy-start(f32[12]{0:T(128)} %constant.61.clone) | copy-start | bytes 148
  169.8 22.9 %all-to-all-start = ((f32[12,64,128]{2,0,1:T(8,128)}), f32[12,64,128]{2,0,1:T(8,128)S(1)}, u32[]{:S(2)}, u32[]{:S(2)}) async-start(f32[12,64,128]{2,0,1:T(8,128)} %copy.85), calls=%async_computation.1 | async-start | bytes 1048576 | tf_op jit(solution)/shard_map/all_to_all | solution.py:137
Sparse Core Ops, SparseCore 0:
  32.9 24.5 all-gather.2
  75.8 19.4 all-gather.4
  121.4 11.9 reduce-scatter.1
where the time goes:
time: 259 us; the launch traced here: 255 us
  other arithmetic  79.3 us (31%)
  waiting for transfers between devices  77.8 us (30%)
  matrix products  46.1 us (18%)
  starting transfers between devices  25.1 us (10%)
  between operations  13.5 us (5%)
  local copies, waits for them, and re-layouts  9.06 us (3%)
  blocking collectives  3.81 us (1%)
    all_gather x2, waiting for transfers between devices, on_device(): lax.all_gather(rim, 'chan', axis=0, tiled=True)  43.9 us
    dot_general x26, matrix products, conv_taps(): jnp.einsum('oc,chw->ohw', taps, window, preferred_element_type=jnp.float32)  33.9 us
    scatter-add x1, other arithmetic, on_device(): sums = jax.ops.segment_sum(share.T, mine, num_segments=owners * basins_here)  30.7 us
    dynamic_update_slice x30, other arithmetic, bucket_run(): final, runoff = lax.scan(day, start, (precip, temp, pet))  22.6 us
    sub x30, other arithmetic, day(): lower = lower - base  21.8 us
    all_to_all x1, waiting for transfers between devices, on_device(): lax.all_to_all(sums, 'tile', split_axis=1, concat_axis=1, tiled=True)  12.6 us
    reduce_scatter x1, waiting for transfers between devices, on_device(): lax.psum_scatter(jnp.einsum('cp,chw->hpw', head_weight, hidden, preferred...  12.1 us
    ppermute x3, starting transfers between devices, padded_2(): lax.ppermute(tail, axis, [(i, (i + 1) % count) for i in range(ends)])  10.5 us
  transfers between devices with their start and end apart: 10, of which 7 were waited for; matrix products, arithmetic and copies ran while one was open for 1% of the time, Pallas kernels for 0%

commit v1 on v0

v1 whole, which is shorter than its diff:
```python
import jax
import jax.numpy as jnp
from jax import lax
from jax.experimental import pallas as pl
from jax.experimental.pallas import tpu as pltpu
from jax.sharding import PartitionSpec as P

LAGS = 15
LOW = [-2.0, 0.5, 50.0, 1.0, 0.3, 0.05, 0.01, 0.001, 0.0, 0.5, 1.0, 0.5]
SPAN = [4.0, 5.5, 450.0, 4.0, 0.7, 0.45, 0.29, 0.099, 50.0, 5.5, 2.0, 2.5]
MESH = pl.DeviceIdType.MESH
F32 = jnp.float32
BF16 = jnp.bfloat16

A = 35
TH = 16
HALF = 8
W = 512
NT = 64
CP = 64
SUB = 16
STEP = W // SUB
WP = W + 2 * SUB
HW0 = 576
TAPS2 = 592
TAPS3 = TAPS2 + 1152
WROWS = TAPS3 + 1152


def dot(a, b):
    return jnp.dot(a, b, preferred_element_type=F32)


def dot_nt(a, b):
    return lax.dot_general(a, b, (((1,), (1,)), ((), ())), preferred_element_type=F32)


def dot_tn(a, b):
    return lax.dot_general(a, b, (((0,), (0,)), ((), ())), preferred_element_type=F32)


def put_row(dst, row, a):
    sub = lax.broadcasted_iota(jnp.int32, (SUB, a.shape[1]), 0)
    dst[row, SUB : SUB + W, :] = a.astype(BF16)
    before = jnp.where(sub == 0, 0.0, pltpu.roll(a[W - SUB :], 1, axis=0))
    after = jnp.where(sub == SUB - 1, 0.0, pltpu.roll(a[:SUB], SUB - 1, axis=0))
    dst[row, :SUB, :] = before.astype(BF16)
    dst[row, SUB + W :, :] = after.astype(BF16)


def raster_kernel(
    attr, cb, w1, w2, w3, hw, out,
    spread, slots, perm, wsend, wrecv, wide1, wide2, wide3, wideh,
    h0, h1, h2, h3, maskb, sendb, recvb, sibb,
    halo_send, halo_recv, w_send, w_recv, row_send, row_recv, sib_send, sib_recv,
):
    tile = lax.axis_index("tile")
    chan = lax.axis_index("chan")
    barrier = pltpu.get_barrier_semaphore()

    def greet(i, carry):
        pl.semaphore_signal(
            barrier, inc=1, device_id={"tile": lax.rem(tile + i, NT)}, device_id_type=MESH
        )
        return carry

    lax.fori_loop(1, NT, greet, 0)
    pl.semaphore_signal(barrier, inc=1, device_id={"chan": 1 - chan}, device_id_type=MESH)

    flat = attr[...].reshape(A * TH, W)
    for g in range(4):
        spread[g, : A * TH, :] = flat[:, g * 128 : (g + 1) * 128].astype(F32)
        spread[g, A * TH :, :] = jnp.zeros((48 * TH - A * TH, 128), F32)
    for r in range(TH):
        for g in range(4):
            part = spread[g, pl.ds(r, 48, stride=TH), :]
            slots[(3 + r) * CP : (3 + r) * CP + 48, g * 128 : (g + 1) * 128] = part.astype(BF16)
        slots[(3 + r) * CP + 48 : (4 + r) * CP, :] = jnp.zeros((CP - 48, W), BF16)

    lane = lax.broadcasted_iota(jnp.int32, (128, 128), 1)
    mine = lane // 64 == chan
    wsend[:TAPS2, :] = jnp.zeros((TAPS2, 128), BF16)
    for t in range(9):
        w = w1[t // 3, t % 3].astype(F32)
        w = jnp.where(mine[:A], jnp.concatenate([w, w], axis=1), 0.0)
        wsend[t * CP : t * CP + A, :] = w.astype(BF16)
    w = hw[...].astype(F32)
    w = jnp.where(mine[:12], jnp.concatenate([w, w], axis=1), 0.0)
    wsend[HW0 : HW0 + 12, :] = w.astype(BF16)
    for base, ref in ((TAPS2, w2), (TAPS3, w3)):
        for t in range(9):
            w = ref[t // 3, t % 3].astype(F32)
            w = jnp.concatenate([w, w], axis=0).T
            wsend[base + t * 128 : base + (t + 1) * 128, :] = jnp.where(mine, w, 0.0).astype(BF16)

    pl.semaphore_wait(barrier, NT)
    other = lax.rem(tile + jnp.where(chan == 0, 1, NT - 1), NT)
    src_at = pl.multiple_of((16 - 13 * chan) * CP, CP)
    dst_at = pl.multiple_of(19 * chan * CP, CP)
    halo = pltpu.make_async_remote_copy(
        src_ref=slots.at[pl.ds(src_at, 3 * CP)],
        dst_ref=slots.at[pl.ds(dst_at, 3 * CP)],
        send_sem=halo_send,
        recv_sem=halo_recv,
        device_id={"tile": other},
        device_id_type=MESH,
    )
    halo.start()
    weights = []
    for k, (first, last) in enumerate(((0, TAPS2), (TAPS2, TAPS3), (TAPS3, WROWS))):
        weights.append(
            pltpu.make_async_remote_copy(
                src_ref=wsend.at[pl.ds(first, last - first)],
                dst_ref=wrecv.at[pl.ds(first, last - first)],
                send_sem=w_send.at[k],
                recv_sem=w_recv.at[k],
                device_id={"chan": 1 - chan},
                device_id_type=MESH,
            )
        )
        weights[-1].start()

    place = lax.broadcasted_iota(jnp.int32, (W, W), 0)
    column = lax.broadcasted_iota(jnp.int32, (W, W), 1)
    perm[...] = ((place % SUB) * STEP + place // SUB == column).astype(F32).astype(BF16)

    def arrange(block):
        at = pl.multiple_of((chan * HALF + 2 * block) * CP, 2 * CP)
        put_row(h0, block, dot_nt(perm[...], slots[pl.ds(at, 2 * CP), :]))

    def arrange_own(i, carry):
        arrange(i + 2 * (1 - chan))
        return carry

    def arrange_halo(i, carry):
        arrange(i + 5 * chan)
        return carry

    lax.fori_loop(0, 5, arrange_own, 0)

    own = cb[pl.ds(pl.multiple_of(chan * HALF, HALF), HALF), :]
    firsts, ids1, ids2, owners = [], [], [], []
    for g in range(4):
        run = own[:, g * 128 : (g + 1) * 128]
        first = run[:, :1]
        last = run[:, 127:]
        firsts.append((run == first).astype(F32))
        owners.append(first // 128)
        ids1.append((first % 128).astype(F32))
        ids2.append((last % 128).astype(F32))
    first_mask = jnp.concatenate(firsts, axis=1)
    spreadm = jnp.broadcast_to(first_mask[:, None, :], (HALF, 16, W)).reshape(HALF * 16, W)
    maskb[...] = dot_nt(perm[...], spreadm.astype(BF16))

    wide1[...] = jnp.zeros(wide1.shape, BF16)
    wide2[...] = jnp.zeros(wide2.shape, BF16)
    wide3[...] = jnp.zeros(wide3.shape, BF16)
    weights[0].wait_recv()
    for t in range(9):
        dy, dx = t // 3, t % 3
        w = wsend[t * CP : (t + 1) * CP, :] + wrecv[t * CP : (t + 1) * CP, :]
        for e in range(2):
            row = dy + e
            at = ((row // 2) * 3 + dx) * 128 + (row % 2) * CP
            wide1[at : at + CP, e * 128 : (e + 1) * 128] = w
    w = (wsend[HW0:TAPS2, :] + wrecv[HW0:TAPS2, :]).astype(F32)
    w = jnp.broadcast_to(w[None], (HALF, 16, 128)).reshape(128, 128).T
    for r in range(HALF):
        wideh[r * 128 : (r + 1) * 128, :] = jnp.where(lane // 16 == r, w, 0.0).astype(BF16)

    halo.wait_recv()
    top = jnp.logical_and(chan == 0, tile == 0)
    bottom = jnp.logical_and(chan == 1, tile == NT - 1)

    @pl.when(jnp.logical_or(top, bottom))
    def _():
        slots[pl.ds(dst_at, 3 * CP), :] = jnp.zeros((3 * CP, W), BF16)

    lax.fori_loop(0, 2, arrange_halo, 0)

    def first_conv(pair, carry):
        lhs = jnp.concatenate(
            [h0[pair + b, dx * SUB : dx * SUB + W, :] for b in range(2) for dx in range(3)], axis=1
        )
        acc = jnp.maximum(dot(lhs, wide1[...]), 0.0)
        put_row(h1, 2 * pair, acc[:, :128])
        put_row(h1, 2 * pair + 1, acc[:, 128:])
        return carry

    lax.fori_loop(0, 6, first_conv, 0)

    @pl.when(top)
    def _():
        h1[0:2] = jnp.zeros((2, WP, 128), BF16)

    @pl.when(bottom)
    def _():
        h1[10:12] = jnp.zeros((2, WP, 128), BF16)

    def widen(k, base, wide):
        weights[k].wait_recv()
        for t in range(9):
            dy, dx = t // 3, t % 3
            span = slice(base + t * 128, base + (t + 1) * 128)
            w = wsend[span, :] + wrecv[span, :]
            for e in range(2):
                at = ((dy + e) * 3 + dx) * 128
                wide[at : at + 128, e * 128 : (e + 1) * 128] = w

    def taps(src, pair):
        return jnp.concatenate(
            [
                src[2 * pair + dy, dx * SUB : dx * SUB + W, :]
                for dy in range(4)
                for dx in range(3)
            ],
            axis=1,
        )

    widen(1, TAPS2, wide2)

    def second_conv(pair, carry):
        acc = jnp.maximum(dot(taps(h1, pair), wide2[...]), 0.0)
        put_row(h2, 2 * pair, acc[:, :128])
        put_row(h2, 2 * pair + 1, acc[:, 128:])
        return carry

    lax.fori_loop(0, 5, second_conv, 0)

    @pl.when(top)
    def _():
        h2[0:1] = jnp.zeros((1, WP, 128), BF16)

    @pl.when(bottom)
    def _():
        h2[9:10] = jnp.zeros((1, WP, 128), BF16)

    widen(2, TAPS3, wide3)

    def third_conv(pair, carry):
        acc = jnp.maximum(dot(taps(h2, pair), wide3[...]), 0.0)
        h3[pair] = acc.astype(BF16)
        return carry

    lax.fori_loop(0, 4, third_conv, 0)

    raw = dot(jnp.concatenate([h3[q] for q in range(4)], axis=1), wideh[...])
    share = jax.nn.sigmoid(raw)
    m = maskb[...]
    part1 = share * m
    part2 = share * (1.0 - m)
    sub32 = lax.broadcasted_iota(jnp.int32, (HALF, 128), 0)
    lane32 = lax.broadcasted_iota(jnp.int32, (HALF, 128), 1)
    rows = []
    for g in range(4):
        pair = []
        for part, ids in ((part1, ids1), (part2, ids2)):
            s = jnp.sum(part.reshape(W // SUB, SUB, 128), axis=0)
            s = jnp.sum(s[4 * g : 4 * g + 4], axis=0, keepdims=True)
            v = jnp.where(lane32 // 16 == sub32, jnp.broadcast_to(s, (HALF, 128)), 0.0)
            for shift in (64, 32, 16):
                v = v + pltpu.roll(v, shift, axis=1)
            pair.append(jnp.where(lane32 % 16 == 12, jnp.broadcast_to(ids[g], (HALF, 128)), v))
        rows.append(jnp.where((lane32 // 16) % 2 == 0, pair[0], pair[1]))
    value = jnp.concatenate(rows, axis=0)
    hi = value.astype(BF16).astype(F32)
    mid = (value - hi).astype(BF16).astype(F32)
    low = value - hi - mid
    kind = lax.broadcasted_iota(jnp.int32, (32, 128), 1) // 32
    parts = jnp.where(kind == 0, hi, jnp.where(kind == 1, mid, jnp.where(kind == 2, low, 0.0)))
    lane128 = lax.broadcasted_iota(jnp.int32, (HALF, 128), 1)
    to_owner = jnp.concatenate(
        [(jnp.broadcast_to(o, (HALF, 128)) == lane128).astype(F32) for o in owners], axis=0
    )
    routed = dot_tn(to_owner.astype(BF16), parts.astype(BF16))[:NT]
    sendb[...] = routed.reshape(NT, 1, 128)
    recvb[tile] = sendb[tile]

    def row_copy(o):
        return pltpu.make_async_remote_copy(
            src_ref=sendb.at[o],
            dst_ref=recvb.at[tile],
            send_sem=row_send,
            recv_sem=row_recv,
            device_id={"tile": o},
            device_id_type=MESH,
        )

    def send_row(i, carry):
        row_copy(lax.rem(tile + i, NT)).start()
        return carry

    lax.fori_loop(1, NT, send_row, 0)
    rest = pl.ds(0, NT - 1)
    pltpu.make_async_copy(recvb.at[rest], recvb.at[rest], row_recv).wait()
    sib = pltpu.make_async_remote_copy(
        src_ref=recvb,
        dst_ref=sibb,
        send_sem=sib_send,
        recv_sem=sib_recv,
        device_id={"chan": 1 - chan},
        device_id_type=MESH,
    )
    sib.start()
    sib.wait_recv()
    got = recvb[...].reshape(NT, 128) + sibb[...].reshape(NT, 128)
    basin = lax.broadcasted_iota(jnp.int32, (NT, 128), 1).astype(F32)
    gotb = got.astype(BF16)
    sums = jnp.zeros((16, 128), F32)
    for b in range(2):
        hit = (jnp.broadcast_to(got[:, 16 * b + 12 : 16 * b + 13], (NT, 128)) == basin).astype(F32)
        placed = dot_tn(gotb, hit.astype(BF16))
        for k in range(3):
            sums = sums + placed[32 * k + 16 * b : 32 * k + 16 * b + 16]
    out[...] = sums

    pltpu.make_async_copy(sendb.at[rest], sendb.at[rest], row_send).wait()
    sib.wait_send()
    halo.wait_send()
    for copy in weights:
        copy.wait_send()


def raster(attributes, cell_basin, w1, w2, w3, hw):
    vmem = pl.BlockSpec(memory_space=pltpu.VMEM)
    return pl.pallas_call(
        raster_kernel,
        out_shape=jax.ShapeDtypeStruct((16, 128), F32),
        in_specs=[vmem] * 6,
        out_specs=vmem,
        scratch_shapes=[
            pltpu.VMEM((4, 48 * TH, 128), F32),
            pltpu.VMEM((22 * CP, W), BF16),
            pltpu.VMEM((W, W), BF16),
            pltpu.VMEM((WROWS, 128), BF16),
            pltpu.VMEM((WROWS, 128), BF16),
            pltpu.VMEM((768, 256), BF16),
            pltpu.VMEM((1536, 256), BF16),
            pltpu.VMEM((1536, 256), BF16),
            pltpu.VMEM((1024, 128), BF16),
            pltpu.VMEM((7, WP, 128), BF16),
            pltpu.VMEM((12, WP, 128), BF16),
            pltpu.VMEM((10, WP, 128), BF16),
            pltpu.VMEM((4, W, 256), BF16),
            pltpu.VMEM((W, 128), F32),
            pltpu.VMEM((NT, 1, 128), F32),
            pltpu.VMEM((NT, 1, 128), F32),
            pltpu.VMEM((NT, 1, 128), F32),
            pltpu.SemaphoreType.DMA,
            pltpu.SemaphoreType.DMA,
            pltpu.SemaphoreType.DMA((3,)),
            pltpu.SemaphoreType.DMA((3,)),
            pltpu.SemaphoreType.DMA,
            pltpu.SemaphoreType.DMA,
            pltpu.SemaphoreType.DMA,
            pltpu.SemaphoreType.DMA,
        ],
        compiler_params=pltpu.CompilerParams(
            collective_id=0, has_side_effects=True, vmem_limit_bytes=48 * 1024 * 1024
        ),
        name="raster",
    )(attributes, cell_basin, w1, w2, w3, hw)


def bucket_kernel(sums, cells, precip, temp, pet, out):
    mean = sums[...] / cells[...].astype(F32)
    shape = (8, 128)
    param = [LOW[p] + SPAN[p] * mean[p : p + 1] for p in range(12)]
    tt, cfmax, fc, beta, lp, k0, k1, k2, uzl, perc = [
        jnp.broadcast_to(param[p], shape) for p in range(10)
    ]
    raw = [
        jnp.exp((param[10] - 1.0) * jnp.log(jnp.float32(k + 0.5)) - (k + 0.5) / param[11])
        for k in range(LAGS)
    ]
    total = raw[0]
    for k in range(1, LAGS):
        total = total + raw[k]
    kernel = [jnp.broadcast_to(r / total, shape) for r in raw]
    dry = lp * fc
    per_dry = 1.0 / dry
    per_fc = 1.0 / fc
    snow = jnp.zeros(shape, F32)
    soil = 0.5 * fc
    upper = jnp.full(shape, 5.0, F32)
    lower = jnp.full(shape, 20.0, F32)
    runoff = []
    for d in range(precip.shape[0]):
        rain, air, demand = precip[d], temp[d], pet[d]
        warm = air - tt
        liquid = jax.nn.sigmoid(warm)
        wet = rain * liquid
        gained = snow + (rain - wet)
        snow = jnp.maximum(gained - cfmax * jnp.maximum(warm, 0.0), 0.0)
        inflow = wet + (gained - snow)
        recharge = inflow * jnp.exp(beta * jnp.log(soil * per_fc))
        soil = soil + inflow - recharge
        excess = jnp.maximum(soil - fc, 0.0)
        soil = soil - excess
        soil = jnp.where(soil < dry, soil * (1.0 - demand * per_dry), soil - demand)
        upper = upper + recharge + excess
        upper_new = jnp.maximum(upper - perc, 0.0)
        lower = lower + upper - upper_new
        quick = k0 * jnp.maximum(upper_new - uzl, 0.0)
        slow = k1 * upper_new
        upper = upper_new - quick - slow
        base = k2 * lower
        lower = lower - base
        runoff.append(quick + slow + base)
        flow = kernel[0] * runoff[d]
        for k in range(1, min(d, LAGS - 1) + 1):
            flow = flow + kernel[k] * runoff[d - k]
        out[d] = flow


def bucket(sums, cells, precip, temp, pet):
    vmem = pl.BlockSpec(memory_space=pltpu.VMEM)
    return pl.pallas_call(
        bucket_kernel,
        out_shape=jax.ShapeDtypeStruct(precip.shape, F32),
        in_specs=[vmem] * 5,
        out_specs=vmem,
        name="bucket",
    )(sums, cells, precip, temp, pet)


def on_device(
    attributes, cell_basin, basin_cells, conv_first, conv_second, conv_third, head_weight,
    precip, temp, pet,
):
    sums = raster(
        attributes,
        cell_basin,
        jnp.transpose(conv_first, (1, 2, 3, 0)),
        jnp.transpose(conv_second, (1, 2, 0, 3)),
        jnp.transpose(conv_third, (1, 2, 0, 3)),
        head_weight.T,
    )
    return bucket(sums, basin_cells.reshape(1, 128), precip, temp, pet)


def solution(mesh):
    return jax.shard_map(
        on_device,
        mesh=mesh,
        in_specs=(
            P(None, "tile", None),
            P("tile", None),
            P("tile"),
            P("chan", None, None, None),
            P("chan", None, None, None),
            P("chan", None, None, None),
            P("chan", None),
            P(None, "chan", "tile"),
            P(None, "chan", "tile"),
            P(None, "chan", "tile"),
        ),
        out_specs=P(None, "chan", "tile"),
        check_vma=False,
    )
```

time: 259 us -> 39.7 us (0.15); the launches traced: 255 us -> 39.4 us
  other arithmetic: 79.3 us -> 0 us
  waiting for transfers between devices: 77.8 us -> 0 us
  matrix products: 46.1 us -> 0 us
  Pallas kernels: 0 us -> 33.5 us
  starting transfers between devices: 25.1 us -> 0 us
  between operations: 13.5 us -> 0.02 us
  blocking collectives: 3.81 us -> 0 us
  local copies, waits for them, and re-layouts: 9.06 us -> 5.81 us
    dot_general x29 -> x0, matrix products: 46.1 us -> none  [the longest x26 33.9 us: conv_taps(): jnp.einsum('oc,chw->ohw', taps, window, preferred_element_type=jnp.float32)]
    all_gather x2 -> x0, waiting for transfers between devices: 43.9 us -> none  [on_device(): lax.all_gather(rim, 'chan', axis=0, tiled=True)]
    pallas_call x0 -> x2, Pallas kernels: none -> 33.5 us  [the longest x1 31.1 us: raster(): pl.pallas_call(raster_kernel, out_shape=jax.ShapeDtypeStruct((16, 128), F...]
    scatter-add x1 -> x0, other arithmetic: 30.7 us -> none  [on_device(): sums = jax.ops.segment_sum(share.T, mine, num_segments=owners * basins_here)]
    dynamic_update_slice x30 -> x0, other arithmetic: 22.6 us -> none  [bucket_run(): final, runoff = lax.scan(day, start, (precip, temp, pet))]
    sub x31 -> x0, other arithmetic: 21.8 us -> none  [the longest x30 21.8 us: day(): lower = lower - base]
    ppermute x6 -> x0, starting transfers between devices: 14.5 us -> none  [the longest x3 10.5 us: padded_2(): lax.ppermute(tail, axis, [(i, (i + 1) % count) for i in range(ends)])]
    all_to_all x1 -> x0, waiting for transfers between devices: 12.6 us -> none  [on_device(): lax.all_to_all(sums, 'tile', split_axis=1, concat_axis=1, tiled=True)]
  transfers between devices with their start and end apart: 10 -> 0, of which waited for: 7 -> 0; matrix products, arithmetic and copies ran while one was open for 1% -> 0% of each run, Pallas kernels for 0% -> 0%
where the time goes in v1:
time: 39.7 us; the launch traced here: 39.4 us
  Pallas kernels  33.5 us (84%)
  local copies, waits for them, and re-layouts  5.81 us (15%)
    pallas_call x1, Pallas kernels, raster(): pl.pallas_call(raster_kernel, out_shape=jax.ShapeDtypeStruct((16, 128), F...  31.1 us
    unnamed x14, local copies, waits for them, and re-layouts  5.81 us
    pallas_call x1, Pallas kernels, bucket(): pl.pallas_call(bucket_kernel, out_shape=jax.ShapeDtypeStruct(precip.shape...  2.42 us

profile of v1, /device:TPU:1, one launch (start us, length us, event | category | flops | bytes accessed | tf_op | source)
XLA Modules:
  0.0 39.4 jit_solution(6263787361116653854)
XLA Ops:
  0.0 0.0 copy-start.6
  0.0 0.7 %copy-done.6 = bf16[64,12]{0,1:T(8,128)(2,1)S(1)} copy-done((bf16[64,12]{0,1:T(8,128)(2,1)S(1)}, bf16[64,12]{0,1:T(8,128)(2,1)}, u32[]{:S(2)}) %copy-start.6) | copy-done | bytes 1560
  0.7 0.0 copy-start
  0.7 1.1 %copy-done = bf16[35,16,512]{2,1,0:T(8,128)(2,1)S(1)} copy-done((bf16[35,16,512]{2,1,0:T(8,128)(2,1)S(1)}, bf16[35,16,512]{2,1,0:T(8,128)(2,1)}, u32[]{:S(2)}) %copy-start) | copy-done | bytes 573464
  1.7 0.0 copy-start.1
  1.7 0.9 %copy-done.1 = bf16[64,3,3,128]{3,0,2,1:T(8,128)(2,1)S(1)} copy-done((bf16[64,3,3,128]{3,0,2,1:T(8,128)(2,1)S(1)}, bf16[64,3,3,128]{3,0,2,1:T(8,128)(2,1)}, u32[]{:S(2)}) %copy-start.1) | copy-done | bytes 147480
  2.7 0.0 copy-start.2
  2.7 0.9 %copy-done.2 = bf16[64,3,3,128]{3,0,2,1:T(8,128)(2,1)S(1)} copy-done((bf16[64,3,3,128]{3,0,2,1:T(8,128)(2,1)S(1)}, bf16[64,3,3,128]{3,0,2,1:T(8,128)(2,1)}, u32[]{:S(2)}) %copy-start.2) | copy-done | bytes 147480
  3.6 0.0 copy-start.3
  3.6 0.9 %copy-done.3 = bf16[64,3,3,35]{0,3,2,1:T(8,128)(2,1)S(1)} copy-done((bf16[64,3,3,35]{0,3,2,1:T(8,128)(2,1)S(1)}, bf16[64,3,3,35]{0,3,2,1:T(8,128)(2,1)}, u32[]{:S(2)}) %copy-start.3) | copy-done | bytes 40344
  4.5 0.0 copy-start.5
  4.5 0.8 %copy-done.5 = s32[16,512]{1,0:T(8,128)S(1)} copy-done((s32[16,512]{1,0:T(8,128)S(1)}, s32[16,512]{1,0:T(8,128)}, u32[]{:S(2)}) %copy-start.5) | copy-done | bytes 32792
  5.2 31.1 %raster.1.sums = f32[16,128]{1,0:T(8,128)S(1)} custom-call(bf16[35,16,512]{2,1,0:T(8,128)(2,1)S(1)} %copy-done, s32[16,512]{1,0:T(8,128)S(1)} %copy-done.5, bf16[3,3,35,64]{3,2,1,0:T(8,128)(2,1)S(1)} %bitcast.7, bf16[3,3,64,128]{3,2,1,0:T(8,128)(2,1)S(1)} %bitcast.5, bf16[3,3,64,128]{3,2,1,0:T(8,128)(2,1)S(1)} %bitcast.6, bf16[12,64]{1,0:T(8,128)(2,1)S(1)} %bitcast.8), custom_call_target="tpu_custom_call" | custom-call | tf_op jit(solution)/shard_map/raster/pallas_call | solution.py:326
  36.3 0.0 copy-start.4
  36.3 0.6 %copy-done.4 = f32[16,128]{1,0:T(8,128)} copy-done((f32[16,128]{1,0:T(8,128)}, f32[16,128]{1,0:T(8,128)S(1)}, u32[]{:S(2)}) %copy-start.4) | copy-done | bytes 8216
  36.9 2.4 %bucket.1 = f32[30,8,128]{2,1,0:T(8,128)} custom-call(f32[16,128]{1,0:T(8,128)} %copy-done.4, s32[1,128]{1,0:T(1,128)} %bitcast.9, f32[30,8,128]{2,1,0:T(8,128)} %precip.1, f32[30,8,128]{2,1,0:T(8,128)} %temp.1, f32[30,8,128]{2,1,0:T(8,128)} %pet.1), custom_call_target="tpu_custom_call" | custom-call | tf_op jit(solution)/shard_map/bucket/pallas_call | solution.py:418
Async XLA Ops:
  0.0 0.7 %copy-start.6 = (bf16[64,12]{0,1:T(8,128)(2,1)S(1)}, bf16[64,12]{0,1:T(8,128)(2,1)}, u32[]{:S(2)}) copy-start(bf16[64,12]{0,1:T(8,128)(2,1)} %param.16) | copy-start | bytes 4612
  0.7 1.1 %copy-start = (bf16[35,16,512]{2,1,0:T(8,128)(2,1)S(1)}, bf16[35,16,512]{2,1,0:T(8,128)(2,1)}, u32[]{:S(2)}) copy-start(bf16[35,16,512]{2,1,0:T(8,128)(2,1)} %attr.1) | copy-start | bytes 1720324
  1.7 0.9 %copy-start.1 = (bf16[64,3,3,128]{3,0,2,1:T(8,128)(2,1)S(1)}, bf16[64,3,3,128]{3,0,2,1:T(8,128)(2,1)}, u32[]{:S(2)}) copy-start(bf16[64,3,3,128]{3,0,2,1:T(8,128)(2,1)} %param.14) | copy-start | bytes 442372
  2.7 0.9 %copy-start.2 = (bf16[64,3,3,128]{3,0,2,1:T(8,128)(2,1)S(1)}, bf16[64,3,3,128]{3,0,2,1:T(8,128)(2,1)}, u32[]{:S(2)}) copy-start(bf16[64,3,3,128]{3,0,2,1:T(8,128)(2,1)} %param.15) | copy-start | bytes 442372
  3.6 0.9 %copy-start.3 = (bf16[64,3,3,35]{0,3,2,1:T(8,128)(2,1)S(1)}, bf16[64,3,3,35]{0,3,2,1:T(8,128)(2,1)}, u32[]{:S(2)}) copy-start(bf16[64,3,3,35]{0,3,2,1:T(8,128)(2,1)} %param.13) | copy-start | bytes 120964
  4.5 0.8 %copy-start.5 = (s32[16,512]{1,0:T(8,128)S(1)}, s32[16,512]{1,0:T(8,128)}, u32[]{:S(2)}) copy-start(s32[16,512]{1,0:T(8,128)} %cb.1) | copy-start | bytes 98308
  36.3 0.6 %copy-start.4 = (f32[16,128]{1,0:T(8,128)}, f32[16,128]{1,0:T(8,128)S(1)}, u32[]{:S(2)}) copy-start(f32[16,128]{1,0:T(8,128)S(1)} %raster.1.sums) | copy-start | bytes 24580

commit v2 on v1

v2 whole, which is shorter than its diff:
```python
import jax
import jax.numpy as jnp
from jax import lax
from jax.experimental import pallas as pl
from jax.experimental.pallas import tpu as pltpu
from jax.sharding import PartitionSpec as P

LAGS = 15
LOW = [-2.0, 0.5, 50.0, 1.0, 0.3, 0.05, 0.01, 0.001, 0.0, 0.5, 1.0, 0.5]
SPAN = [4.0, 5.5, 450.0, 4.0, 0.7, 0.45, 0.29, 0.099, 50.0, 5.5, 2.0, 2.5]
MESH = pl.DeviceIdType.MESH
F32 = jnp.float32
BF16 = jnp.bfloat16

A = 35
TH = 16
HALF = 8
W = 512
NT = 64
CP = 64
SUB = 16
STEP = W // SUB
WP = W + 2 * SUB


def dot(a, b):
    return jnp.dot(a, b, preferred_element_type=F32)


def dot_nt(a, b):
    return lax.dot_general(a, b, (((1,), (1,)), ((), ())), preferred_element_type=F32)


def dot_tn(a, b):
    return lax.dot_general(a, b, (((0,), (0,)), ((), ())), preferred_element_type=F32)


def put_row(dst, row, a):
    sub = lax.broadcasted_iota(jnp.int32, (SUB, a.shape[1]), 0)
    dst[row, SUB : SUB + W, :] = a.astype(BF16)
    before = jnp.where(sub == 0, 0.0, pltpu.roll(a[W - SUB :], 1, axis=0))
    after = jnp.where(sub == SUB - 1, 0.0, pltpu.roll(a[:SUB], SUB - 1, axis=0))
    dst[row, :SUB, :] = before.astype(BF16)
    dst[row, SUB + W :, :] = after.astype(BF16)


def digits(value):
    return [value // 2**k % 2 for k in (5, 4, 3, 2, 1, 0)]


def greet_order(tile):
    y1, y0, z1, z0, x1, x0 = digits(tile)
    return ((((y1 * 2 + z1) * 2 + x1) * 2 + y0) * 2 + z0) * 2 + x0


def greet_tile(place):
    y1, z1, x1, y0, z0, x0 = digits(place)
    return ((((y1 * 2 + y0) * 2 + z1) * 2 + z0) * 2 + x1) * 2 + x0


def signal(sem, **where):
    pl.semaphore_signal(sem, inc=1, device_id=where, device_id_type=MESH)


def line_peers(tile):
    lines = []
    for weight in (1, 4, 16):
        at = lax.rem(tile // weight, 4)
        lines.append([tile + (lax.rem(at + k, 4) - at) * weight for k in range(1, 4)])
    return lines


def raster_kernel(
    attr_in, cb_in, cells_in, w1_in, w2_in, w3_in, hw_in, precip_in, temp_in, pet_in, out,
    attr, cb, cells, w1, w2, w3, hw, precip, temp, pet, w1r, w2r, w3r, hwr,
    spread, slots, perm, wide1, wide2, wide3, wideh, h0, h1, h2, h3, sendb, recvb,
    local_sems, halo_send, halo_recv, w_send, w_recv, row_send, row_recv,
    z_sem, y_sem, c_sem,
):
    tile = lax.axis_index("tile")
    chan = lax.axis_index("chan")
    barrier = pltpu.get_barrier_semaphore()
    locals_ = [
        pltpu.make_async_copy(src, dst, local_sems.at[k])
        for k, (src, dst) in enumerate(
            (
                (attr_in, attr), (w1_in, w1), (hw_in, hw), (cb_in, cb), (w2_in, w2), (w3_in, w3),
                (cells_in, cells), (precip_in, precip), (temp_in, temp), (pet_in, pet),
            )
        )
    ]
    for copy in locals_:
        copy.start()
    got_attr, got_w1, got_hw, got_cb, got_w2, got_w3 = locals_[:6]

    step = jnp.where(chan == 0, 1, NT - 1)
    towards = lax.rem(tile + step, NT)
    source = lax.rem(tile + NT - step, NT)
    signal(barrier, chan=1 - chan)
    signal(barrier, tile=source)
    x_peers, z_peers, y_peers = line_peers(tile)
    for peer in x_peers + z_peers + y_peers:
        signal(barrier, tile=peer)

    place = lax.broadcasted_iota(jnp.int32, (W, W), 0)
    column = lax.broadcasted_iota(jnp.int32, (W, W), 1)
    perm[...] = ((place % SUB) * STEP + place // SUB == column).astype(F32).astype(BF16)
    wide1[...] = jnp.zeros(wide1.shape, BF16)
    wideh[...] = jnp.zeros(wideh.shape, BF16)
    for wide in (wide2, wide3):
        wide[0:128, 1152:1536] = jnp.zeros((128, 384), BF16)
        wide[128:256, 0:384] = jnp.zeros((128, 384), BF16)

    def place_rows(first, last):
        for r in range(first, last):
            for g in range(4):
                part = spread[g, pl.ds(r, 48, stride=TH), :]
                slots[(3 + r) * CP : (3 + r) * CP + 48, g * 128 : (g + 1) * 128] = part.astype(BF16)
            slots[(3 + r) * CP + 48 : (4 + r) * CP, :] = jnp.zeros((CP - 48, W), BF16)

    got_attr.wait()
    flat = attr[...].reshape(A * TH, W)
    for g in range(4):
        spread[g, : A * TH, :] = flat[:, g * 128 : (g + 1) * 128].astype(F32)
        spread[g, A * TH :, :] = jnp.zeros((48 * TH - A * TH, 128), F32)
    place_rows(0, 3)
    place_rows(13, 16)

    pl.semaphore_wait(barrier, 11)
    src_at = pl.multiple_of((16 - 13 * chan) * CP, CP)
    dst_at = pl.multiple_of(19 * chan * CP, CP)
    halo = pltpu.make_async_remote_copy(
        src_ref=slots.at[pl.ds(src_at, 3 * CP)],
        dst_ref=slots.at[pl.ds(dst_at, 3 * CP)],
        send_sem=halo_send,
        recv_sem=halo_recv,
        device_id={"tile": towards},
        device_id_type=MESH,
    )
    halo.start()
    weights = [
        pltpu.make_async_remote_copy(
            src_ref=src,
            dst_ref=dst,
            send_sem=w_send.at[k],
            recv_sem=w_recv.at[k],
            device_id={"chan": 1 - chan},
            device_id_type=MESH,
        )
        for k, (src, dst) in enumerate(((w1_in, w1r), (hw_in, hwr), (w2_in, w2r), (w3_in, w3r)))
    ]
    for copy in weights:
        copy.start()
    for peer in z_peers:
        signal(z_sem, tile=peer)
    place_rows(3, 13)

    def arrange(block, count):
        at = pl.multiple_of((chan * HALF + 2 * block) * CP, 2 * CP)
        a = dot_nt(perm[...], slots[pl.ds(at, count * 2 * CP), :])
        for k in range(count):
            put_row(h0, block + k, a[:, k * 128 : (k + 1) * 128])

    first_own = 2 * (1 - chan)
    arrange(first_own, 2)
    arrange(first_own + 2, 2)
    arrange(first_own + 4, 1)

    sub8 = lax.broadcasted_iota(jnp.int32, (HALF, 128), 0)
    lane8 = lax.broadcasted_iota(jnp.int32, (HALF, 128), 1)
    sub16 = lax.broadcasted_iota(jnp.int32, (SUB, 128), 0)
    got_cb.wait()
    own = cb[pl.ds(pl.multiple_of(chan * HALF, HALF), HALF), :]
    ids1, ids2, owners = [], [], []
    limit = jnp.zeros((SUB, 128), F32)
    for g in range(4):
        run = own[:, g * 128 : (g + 1) * 128]
        first = run[:, :1]
        last = run[:, 127:]
        count = jnp.sum((run == first).astype(F32), axis=1, keepdims=True)
        count = jnp.where(lane8 // 16 == sub8, jnp.broadcast_to(count, (HALF, 128)), 0.0)
        count = jnp.sum(count, axis=0, keepdims=True)
        limit = jnp.where(sub16 // 4 == g, jnp.broadcast_to(count, (SUB, 128)), limit)
        owners.append(first // 128)
        ids1.append((first % 128).astype(F32))
        ids2.append((last % 128).astype(F32))
    limit = limit - ((sub16 % 4) * STEP).astype(F32)

    def widen(mine, theirs, wide):
        for half, ref in ((chan, mine), (1 - chan, theirs)):
            for t in range(9):
                dy, dx = t // 3, t % 3
                w = ref[dy, dx]
                for e in range(2):
                    at = ((dy + e) * 3 + dx) * 128
                    wide[pl.ds(pl.multiple_of(e * 128 + half * 64, 64), 64), at : at + 128] = w

    def both(mine, theirs):
        left = jnp.where(chan == 0, mine, theirs)
        right = jnp.where(chan == 0, theirs, mine)
        return jnp.concatenate([left, right], axis=1)

    got_w1.wait()
    weights[0].wait_recv()
    for t in range(9):
        dy, dx = t // 3, t % 3
        w = both(w1[dy, dx].astype(F32), w1r[dy, dx].astype(F32)).astype(BF16)
        for e in range(2):
            row = dy + e
            at = ((row // 2) * 3 + dx) * 128 + (row % 2) * CP
            wide1[at : at + A, e * 128 : (e + 1) * 128] = w

    top = jnp.logical_and(chan == 0, tile == 0)
    bottom = jnp.logical_and(chan == 1, tile == NT - 1)
    halo.wait_recv()

    @pl.when(jnp.logical_or(top, bottom))
    def _():
        slots[pl.ds(dst_at, 3 * CP), :] = jnp.zeros((3 * CP, W), BF16)

    arrange(5 * chan, 2)

    for pair in range(6):
        lhs = jnp.concatenate(
            [h0[pair + b, dx * SUB : dx * SUB + W, :] for b in range(2) for dx in range(3)], axis=1
        )
        acc = jnp.maximum(dot(lhs, wide1[...]), 0.0)
        put_row(h1, 2 * pair, acc[:, :128])
        put_row(h1, 2 * pair + 1, acc[:, 128:])

    @pl.when(top)
    def _():
        h1[0:2] = jnp.zeros((2, WP, 128), BF16)

    @pl.when(bottom)
    def _():
        h1[10:12] = jnp.zeros((2, WP, 128), BF16)

    def taps(src, pair):
        return jnp.concatenate(
            [
                src[2 * pair + dy, dx * SUB : dx * SUB + W, :]
                for dy in range(4)
                for dx in range(3)
            ],
            axis=1,
        )

    pl.semaphore_wait(z_sem, 3)
    for peer in y_peers:
        signal(y_sem, tile=peer)
    got_w2.wait()
    weights[2].wait_recv()
    widen(w2, w2r, wide2)
    for pair in range(5):
        acc = jnp.maximum(dot_nt(taps(h1, pair), wide2[...]), 0.0)
        put_row(h2, 2 * pair, acc[:, :128])
        put_row(h2, 2 * pair + 1, acc[:, 128:])

    @pl.when(top)
    def _():
        h2[0:1] = jnp.zeros((1, WP, 128), BF16)

    @pl.when(bottom)
    def _():
        h2[9:10] = jnp.zeros((1, WP, 128), BF16)

    pl.semaphore_wait(y_sem, 3)
    signal(c_sem, chan=1 - chan)
    got_w3.wait()
    weights[3].wait_recv()
    widen(w3, w3r, wide3)
    for pair in range(4):
        acc = jnp.maximum(dot_nt(taps(h2, pair), wide3[...]), 0.0)
        h3[:, pair * 256 : (pair + 1) * 256] = acc.astype(BF16)

    got_hw.wait()
    weights[1].wait_recv()
    w = both(hw[...].astype(F32), hwr[...].astype(F32)).astype(BF16)
    for r in range(HALF):
        wideh[r * 16 : r * 16 + 12, r * 128 : (r + 1) * 128] = w
    share = jax.nn.sigmoid(dot_nt(h3[...], wideh[...]))
    sums = [jnp.zeros((SUB, 128), F32), jnp.zeros((SUB, 128), F32)]
    for j in range(STEP):
        v = share[j * SUB : (j + 1) * SUB]
        inside = limit > j
        sums[0] = sums[0] + jnp.where(inside, v, 0.0)
        sums[1] = sums[1] + jnp.where(inside, 0.0, v)
    rows = []
    for g in range(4):
        pair = []
        for s, ids in zip(sums, (ids1, ids2)):
            v = jnp.sum(s[4 * g : 4 * g + 4], axis=0, keepdims=True)
            v = jnp.where(lane8 // 16 == sub8, jnp.broadcast_to(v, (HALF, 128)), 0.0)
            for shift in (64, 32, 16):
                v = v + pltpu.roll(v, shift, axis=1)
            pair.append(jnp.where(lane8 % 16 == 12, jnp.broadcast_to(ids[g], (HALF, 128)), v))
        rows.append(jnp.where((lane8 // 16) % 2 == 0, pair[0], pair[1]))
    value = jnp.concatenate(rows, axis=0)
    hi = value.astype(BF16).astype(F32)
    mid = (value - hi).astype(BF16).astype(F32)
    low = value - hi - mid
    kind = lax.broadcasted_iota(jnp.int32, (32, 128), 1) // 32
    parts = jnp.where(kind == 0, hi, jnp.where(kind == 1, mid, jnp.where(kind == 2, low, 0.0)))
    to_owner = jnp.concatenate(
        [(jnp.broadcast_to(o, (HALF, 128)) == lane8).astype(F32) for o in owners], axis=0
    )
    routed = dot_tn(to_owner.astype(BF16), parts.astype(BF16))[:NT]
    sendb[...] = routed.reshape(NT, 1, 128)

    pl.semaphore_wait(c_sem, 1)
    me = chan * NT + tile
    recvb[me] = sendb[tile]
    mine_at = greet_order(tile) * 2 + chan
    for i in range(2 * NT - 1):
        swap = mine_at == i
        o = jnp.where(swap, NT - 1, greet_tile(i // 2))
        pltpu.make_async_remote_copy(
            src_ref=sendb.at[o],
            dst_ref=recvb.at[me],
            send_sem=row_send,
            recv_sem=row_recv,
            device_id={"tile": o, "chan": jnp.where(swap, 1, i % 2)},
            device_id_type=MESH,
        ).start()
    rest = pl.ds(0, 2 * NT - 1)
    pltpu.make_async_copy(recvb.at[rest], recvb.at[rest], row_recv).wait()
    got = recvb[...].reshape(2, NT, 128)
    got = got[0] + got[1]
    basin = lax.broadcasted_iota(jnp.int32, (NT, 128), 1).astype(F32)
    gotb = got.astype(BF16)
    total = jnp.zeros((16, 128), F32)
    for b in range(2):
        hit = (jnp.broadcast_to(got[:, 16 * b + 12 : 16 * b + 13], (NT, 128)) == basin).astype(F32)
        placed = dot_tn(gotb, hit.astype(BF16))
        for k in range(3):
            total = total + placed[32 * k + 16 * b : 32 * k + 16 * b + 16]

    for copy in locals_[6:]:
        copy.wait()
    bucket(total, cells[...], precip, temp, pet, out)

    pltpu.make_async_copy(recvb.at[rest], recvb.at[rest], row_send).wait()
    halo.wait_send()
    for copy in weights:
        copy.wait_send()


def bucket(sums, cells, precip, temp, pet, out):
    mean = sums / cells.astype(F32)
    shape = (8, 128)
    param = [LOW[p] + SPAN[p] * mean[p : p + 1] for p in range(12)]
    tt, cfmax, fc, beta, lp, k0, k1, k2, uzl, perc = [
        jnp.broadcast_to(param[p], shape) for p in range(10)
    ]
    raw = [
        jnp.exp((param[10] - 1.0) * jnp.log(jnp.float32(k + 0.5)) - (k + 0.5) / param[11])
        for k in range(LAGS)
    ]
    total = raw[0]
    for k in range(1, LAGS):
        total = total + raw[k]
    kernel = [jnp.broadcast_to(r / total, shape) for r in raw]
    dry = lp * fc
    per_dry = 1.0 / dry
    per_fc = 1.0 / fc
    snow = jnp.zeros(shape, F32)
    soil = 0.5 * fc
    upper = jnp.full(shape, 5.0, F32)
    lower = jnp.full(shape, 20.0, F32)
    runoff = []
    for d in range(precip.shape[0]):
        rain, air, demand = precip[d], temp[d], pet[d]
        warm = air - tt
        liquid = jax.nn.sigmoid(warm)
        wet = rain * liquid
        gained = snow + (rain - wet)
        snow = jnp.maximum(gained - cfmax * jnp.maximum(warm, 0.0), 0.0)
        inflow = wet + (gained - snow)
        recharge = inflow * jnp.exp(beta * jnp.log(soil * per_fc))
        soil = soil + inflow - recharge
        excess = jnp.maximum(soil - fc, 0.0)
        soil = soil - excess
        soil = jnp.where(soil < dry, soil * (1.0 - demand * per_dry), soil - demand)
        upper = upper + recharge + excess
        upper_new = jnp.maximum(upper - perc, 0.0)
        lower = lower + upper - upper_new
        quick = k0 * jnp.maximum(upper_new - uzl, 0.0)
        slow = k1 * upper_new
        upper = upper_new - quick - slow
        base = k2 * lower
        lower = lower - base
        runoff.append(quick + slow + base)
        flow = kernel[0] * runoff[d]
        for k in range(1, min(d, LAGS - 1) + 1):
            flow = flow + kernel[k] * runoff[d - k]
        out[d] = flow


def on_device(
    attributes, cell_basin, basin_cells, conv_first, conv_second, conv_third, head_weight,
    precip, temp, pet,
):
    args = (
        attributes,
        cell_basin,
        basin_cells.reshape(1, 128),
        jnp.transpose(conv_first, (1, 2, 3, 0)),
        jnp.transpose(conv_second, (1, 2, 0, 3)),
        jnp.transpose(conv_third, (1, 2, 0, 3)),
        head_weight.T,
        precip,
        temp,
        pet,
    )
    held = [pltpu.VMEM(a.shape, a.dtype) for a in args]
    theirs = [pltpu.VMEM(args[k].shape, BF16) for k in (3, 4, 5, 6)]
    return pl.pallas_call(
        raster_kernel,
        out_shape=jax.ShapeDtypeStruct(precip.shape, F32),
        in_specs=[pl.BlockSpec(memory_space=pltpu.HBM)] * len(args),
        out_specs=pl.BlockSpec(memory_space=pltpu.VMEM),
        scratch_shapes=held
        + theirs
        + [
            pltpu.VMEM((4, 48 * TH, 128), F32),
            pltpu.VMEM((22 * CP, W), BF16),
            pltpu.VMEM((W, W), BF16),
            pltpu.VMEM((768, 256), BF16),
            pltpu.VMEM((256, 1536), BF16),
            pltpu.VMEM((256, 1536), BF16),
            pltpu.VMEM((128, 1024), BF16),
            pltpu.VMEM((7, WP, 128), BF16),
            pltpu.VMEM((12, WP, 128), BF16),
            pltpu.VMEM((10, WP, 128), BF16),
            pltpu.VMEM((W, 1024), BF16),
            pltpu.VMEM((NT, 1, 128), F32),
            pltpu.VMEM((2 * NT, 1, 128), F32),
            pltpu.SemaphoreType.DMA((10,)),
            pltpu.SemaphoreType.DMA,
            pltpu.SemaphoreType.DMA,
            pltpu.SemaphoreType.DMA((4,)),
            pltpu.SemaphoreType.DMA((4,)),
            pltpu.SemaphoreType.DMA,
            pltpu.SemaphoreType.DMA,
            pltpu.SemaphoreType.REGULAR,
            pltpu.SemaphoreType.REGULAR,
            pltpu.SemaphoreType.REGULAR,
        ],
        compiler_params=pltpu.CompilerParams(
            collective_id=0, has_side_effects=True, vmem_limit_bytes=56 * 1024 * 1024
        ),
        name="raster",
    )(*args)


def solution(mesh):
    return jax.shard_map(
        on_device,
        mesh=mesh,
        in_specs=(
            P(None, "tile", None),
            P("tile", None),
            P("tile"),
            P("chan", None, None, None),
            P("chan", None, None, None),
            P("chan", None, None, None),
            P("chan", None),
            P(None, "chan", "tile"),
            P(None, "chan", "tile"),
            P(None, "chan", "tile"),
        ),
        out_specs=P(None, "chan", "tile"),
        check_vma=False,
    )
```

time: 39.7 us -> 31.5 us (0.79)
  local copies, waits for them, and re-layouts: 5.81 us -> 1.56 us
  Pallas kernels: 33.5 us -> 29.8 us
    unnamed x14 -> x1, local copies, waits for them, and re-layouts: 5.81 us -> 1.56 us
    pallas_call x2 -> x1, Pallas kernels: 33.5 us -> 29.8 us  [on_device(): pl.pallas_call(raster_kernel, out_shape=jax.ShapeDtypeStruct(precip.shape...]
where the time goes in v2:
time: 31.5 us; the launch traced here: 31.4 us
  Pallas kernels  29.8 us (95%)
  local copies, waits for them, and re-layouts  1.56 us (5%)
    pallas_call x1, Pallas kernels, on_device(): pl.pallas_call(raster_kernel, out_shape=jax.ShapeDtypeStruct(precip.shape...  29.8 us
    unnamed x1, local copies, waits for them, and re-layouts  1.56 us

profile of v2, /device:TPU:1, one launch (start us, length us, event | category | flops | bytes accessed | tf_op | source)
XLA Modules:
  0.0 31.4 jit_solution(9486672566498894796)
XLA Ops:
  0.0 29.8 %raster.1 = f32[30,8,128]{2,1,0:T(8,128)} custom-call(bf16[35,16,512]{2,1,0:T(8,128)(2,1)} %attr_in.1, s32[16,512]{1,0:T(8,128)} %cb_in.1, s32[1,128]{1,0:T(1,128)} %bitcast.9, bf16[3,3,35,64]{3,2,1,0:T(8,128)(2,1)} %bitcast.7, bf16[3,3,64,128]{3,2,1,0:T(8,128)(2,1)} %bitcast.5, bf16[3,3,64,128]{3,2,1,0:T(8,128)(2,1)} %bitcast.6, bf16[12,64]{1,0:T(8,128)(2,1)} %bitcast.8, ...), custom_call_target="tpu_custom_call" | custom-call | tf_op jit(solution)/shard_map/raster/pallas_call | solution.py:418
  29.8 1.6 %copy.12 = f32[30,8,128]{2,1,0:T(8,128)} copy(f32[30,8,128]{2,1,0:T(8,128)} %raster.1) | data formatting | bytes 245760

commit v3 on v2

--- a/solution.py
+++ b/solution.py
@@ -44,6 +44,12 @@
     dst[row, SUB + W :, :] = after.astype(BF16)
 
 
+def put_pair(dst, pair, a, keep):
+    for e in range(2):
+        row = a[:, e * 128 : (e + 1) * 128]
+        put_row(dst, 2 * pair + e, row if keep is None else row * keep[e])
+
+
 def digits(value):
     return [value // 2**k % 2 for k in (5, 4, 3, 2, 1, 0)]
 
@@ -75,7 +81,7 @@
     attr, cb, cells, w1, w2, w3, hw, precip, temp, pet, w1r, w2r, w3r, hwr,
     spread, slots, perm, wide1, wide2, wide3, wideh, h0, h1, h2, h3, sendb, recvb,
     local_sems, halo_send, halo_recv, w_send, w_recv, row_send, row_recv,
-    z_sem, y_sem, c_sem,
+    z_sem, y_sem,
 ):
     tile = lax.axis_index("tile")
     chan = lax.axis_index("chan")
@@ -93,12 +99,20 @@
         copy.start()
     got_attr, got_w1, got_hw, got_cb, got_w2, got_w3 = locals_[:6]
 
-    step = jnp.where(chan == 0, 1, NT - 1)
-    towards = lax.rem(tile + step, NT)
-    source = lax.rem(tile + NT - step, NT)
+    edge = jnp.where(chan == 0, 0, NT - 1)
+    far = NT - 1 - edge
+    step = 1 - 2 * chan
+    lacks = tile == edge
+    gives = tile != far
+    towards = jnp.where(gives, tile + step, tile - step)
+    source = jnp.where(lacks, tile + step, tile - step)
     signal(barrier, chan=1 - chan)
-    signal(barrier, tile=source)
     x_peers, z_peers, y_peers = line_peers(tile)
+
+    @pl.when(jnp.logical_not(lacks))
+    def _():
+        signal(barrier, tile=source)
+
     for peer in x_peers + z_peers + y_peers:
         signal(barrier, tile=peer)
 
@@ -112,32 +126,14 @@
         wide[128:256, 0:384] = jnp.zeros((128, 384), BF16)
 
     def place_rows(first, last):
-        for r in range(first, last):
+        for i in range(first, last):
+            r = jnp.where(chan == 0, i, TH - 1 - i)
             for g in range(4):
                 part = spread[g, pl.ds(r, 48, stride=TH), :]
-                slots[(3 + r) * CP : (3 + r) * CP + 48, g * 128 : (g + 1) * 128] = part.astype(BF16)
-            slots[(3 + r) * CP + 48 : (4 + r) * CP, :] = jnp.zeros((CP - 48, W), BF16)
-
-    got_attr.wait()
-    flat = attr[...].reshape(A * TH, W)
-    for g in range(4):
-        spread[g, : A * TH, :] = flat[:, g * 128 : (g + 1) * 128].astype(F32)
-        spread[g, A * TH :, :] = jnp.zeros((48 * TH - A * TH, 128), F32)
-    place_rows(0, 3)
-    place_rows(13, 16)
-
-    pl.semaphore_wait(barrier, 11)
-    src_at = pl.multiple_of((16 - 13 * chan) * CP, CP)
-    dst_at = pl.multiple_of(19 * chan * CP, CP)
-    halo = pltpu.make_async_remote_copy(
-        src_ref=slots.at[pl.ds(src_at, 3 * CP)],
-        dst_ref=slots.at[pl.ds(dst_at, 3 * CP)],
-        send_sem=halo_send,
-        recv_sem=halo_recv,
-        device_id={"tile": towards},
-        device_id_type=MESH,
-    )
-    halo.start()
+                slots[(3 + i) * CP : (3 + i) * CP + 48, g * 128 : (g + 1) * 128] = part.astype(BF16)
+            slots[(3 + i) * CP + 48 : (4 + i) * CP, :] = jnp.zeros((CP - 48, W), BF16)
+
+    pl.semaphore_wait(barrier, 10 + gives.astype(jnp.int32))
     weights = [
         pltpu.make_async_remote_copy(
             src_ref=src,
@@ -153,21 +149,45 @@
         copy.start()
     for peer in z_peers:
         signal(z_sem, tile=peer)
-    place_rows(3, 13)
+
+    got_attr.wait()
+    flat = attr[...].reshape(A * TH, W)
+    for g in range(4):
+        spread[g, : A * TH, :] = flat[:, g * 128 : (g + 1) * 128].astype(F32)
+        spread[g, A * TH :, :] = jnp.zeros((48 * TH - A * TH, 128), F32)
+    place_rows(13, 16)
+    halo = pltpu.make_async_remote_copy(
+        src_ref=slots.at[pl.ds(16 * CP, 3 * CP)],
+        dst_ref=slots.at[pl.ds(0, 3 * CP)],
+        send_sem=halo_send,
+        recv_sem=halo_recv,
+        device_id={"tile": towards},
+        device_id_type=MESH,
+    )
+
+    @pl.when(gives)
+    def _():
+        halo.start()
+
+    @pl.when(lacks)
+    def _():
+        slots[: 3 * CP, :] = jnp.zeros((3 * CP, W), BF16)
+
+    place_rows(0, 11)
 
     def arrange(block, count):
-        at = pl.multiple_of((chan * HALF + 2 * block) * CP, 2 * CP)
-        a = dot_nt(perm[...], slots[pl.ds(at, count * 2 * CP), :])
+        at = 2 * block * CP
+        a = dot_nt(perm[...], slots[at : at + count * 2 * CP, :])
         for k in range(count):
             put_row(h0, block + k, a[:, k * 128 : (k + 1) * 128])
 
-    first_own = 2 * (1 - chan)
-    arrange(first_own, 2)
-    arrange(first_own + 2, 2)
-    arrange(first_own + 4, 1)
+    arrange(2, 2)
+    arrange(4, 2)
+    arrange(6, 1)
 
     sub8 = lax.broadcasted_iota(jnp.int32, (HALF, 128), 0)
     lane8 = lax.broadcasted_iota(jnp.int32, (HALF, 128), 1)
+    mine8 = lane8 // 16 == jnp.where(chan == 0, sub8, HALF - 1 - sub8)
     sub16 = lax.broadcasted_iota(jnp.int32, (SUB, 128), 0)
     got_cb.wait()
     own = cb[pl.ds(pl.multiple_of(chan * HALF, HALF), HALF), :]
@@ -178,7 +198,7 @@
         first = run[:, :1]
         last = run[:, 127:]
         count = jnp.sum((run == first).astype(F32), axis=1, keepdims=True)
-        count = jnp.where(lane8 // 16 == sub8, jnp.broadcast_to(count, (HALF, 128)), 0.0)
+        count = jnp.where(mine8, jnp.broadcast_to(count, (HALF, 128)), 0.0)
         count = jnp.sum(count, axis=0, keepdims=True)
         limit = jnp.where(sub16 // 4 == g, jnp.broadcast_to(count, (SUB, 128)), limit)
         owners.append(first // 128)
@@ -190,7 +210,7 @@
         for half, ref in ((chan, mine), (1 - chan, theirs)):
             for t in range(9):
                 dy, dx = t // 3, t % 3
-                w = ref[dy, dx]
+                w = ref[jnp.where(chan == 0, dy, 2 - dy), dx]
                 for e in range(2):
                     at = ((dy + e) * 3 + dx) * 128
                     wide[pl.ds(pl.multiple_of(e * 128 + half * 64, 64), 64), at : at + 128] = w
@@ -200,41 +220,23 @@
         right = jnp.where(chan == 0, theirs, mine)
         return jnp.concatenate([left, right], axis=1)
 
-    got_w1.wait()
-    weights[0].wait_recv()
+    for copy in (got_w1, got_w2, got_w3, got_hw):
+        copy.wait()
+    for copy in weights:
+        copy.wait_recv()
     for t in range(9):
         dy, dx = t // 3, t % 3
-        w = both(w1[dy, dx].astype(F32), w1r[dy, dx].astype(F32)).astype(BF16)
+        at = jnp.where(chan == 0, dy, 2 - dy)
+        w = both(w1[at, dx].astype(F32), w1r[at, dx].astype(F32)).astype(BF16)
         for e in range(2):
             row = dy + e
             at = ((row // 2) * 3 + dx) * 128 + (row % 2) * CP
             wide1[at : at + A, e * 128 : (e + 1) * 128] = w
-
-    top = jnp.logical_and(chan == 0, tile == 0)
-    bottom = jnp.logical_and(chan == 1, tile == NT - 1)
-    halo.wait_recv()
-
-    @pl.when(jnp.logical_or(top, bottom))
-    def _():
-        slots[pl.ds(dst_at, 3 * CP), :] = jnp.zeros((3 * CP, W), BF16)
-
-    arrange(5 * chan, 2)
-
-    for pair in range(6):
-        lhs = jnp.concatenate(
-            [h0[pair + b, dx * SUB : dx * SUB + W, :] for b in range(2) for dx in range(3)], axis=1
-        )
-        acc = jnp.maximum(dot(lhs, wide1[...]), 0.0)
-        put_row(h1, 2 * pair, acc[:, :128])
-        put_row(h1, 2 * pair + 1, acc[:, 128:])
-
-    @pl.when(top)
-    def _():
-        h1[0:2] = jnp.zeros((2, WP, 128), BF16)
-
-    @pl.when(bottom)
-    def _():
-        h1[10:12] = jnp.zeros((2, WP, 128), BF16)
+    widen(w2, w2r, wide2)
+    widen(w3, w3r, wide3)
+    w = both(hw[...].astype(F32), hwr[...].astype(F32)).astype(BF16)
+    for r in range(HALF):
+        wideh[r * 16 : r * 16 + 12, r * 128 : (r + 1) * 128] = w
 
     def taps(src, pair):
         return jnp.concatenate(
@@ -246,40 +248,46 @@
             axis=1,
         )
 
+    def conv1(pair, keep=None):
+        lhs = jnp.concatenate(
+            [h0[pair + b, dx * SUB : dx * SUB + W, :] for b in range(2) for dx in range(3)], axis=1
+        )
+        put_pair(h1, pair, jnp.maximum(dot(lhs, wide1[...]), 0.0), keep)
+
+    def conv2(pair, keep=None):
+        put_pair(h2, pair, jnp.maximum(dot_nt(taps(h1, pair), wide2[...]), 0.0), keep)
+
+    def conv3(pair):
+        h3[pair] = jnp.maximum(dot_nt(taps(h2, pair), wide3[...]), 0.0).astype(BF16)
+
+    for pair in range(2, 6):
+        conv1(pair)
+    for pair in range(2, 5):
+        conv2(pair)
     pl.semaphore_wait(z_sem, 3)
     for peer in y_peers:
         signal(y_sem, tile=peer)
-    got_w2.wait()
-    weights[2].wait_recv()
-    widen(w2, w2r, wide2)
-    for pair in range(5):
-        acc = jnp.maximum(dot_nt(taps(h1, pair), wide2[...]), 0.0)
-        put_row(h2, 2 * pair, acc[:, :128])
-        put_row(h2, 2 * pair + 1, acc[:, 128:])
-
-    @pl.when(top)
+        signal(y_sem, tile=peer, chan=1 - chan)
+    signal(y_sem, chan=1 - chan)
+    for pair in range(2, 4):
+        conv3(pair)
+
+    @pl.when(jnp.logical_not(lacks))
     def _():
-        h2[0:1] = jnp.zeros((1, WP, 128), BF16)
-
-    @pl.when(bottom)
-    def _():
-        h2[9:10] = jnp.zeros((1, WP, 128), BF16)
-
-    pl.semaphore_wait(y_sem, 3)
-    signal(c_sem, chan=1 - chan)
-    got_w3.wait()
-    weights[3].wait_recv()
-    widen(w3, w3r, wide3)
-    for pair in range(4):
-        acc = jnp.maximum(dot_nt(taps(h2, pair), wide3[...]), 0.0)
-        h3[:, pair * 256 : (pair + 1) * 256] = acc.astype(BF16)
-
-    got_hw.wait()
-    weights[1].wait_recv()
-    w = both(hw[...].astype(F32), hwr[...].astype(F32)).astype(BF16)
-    for r in range(HALF):
-        wideh[r * 16 : r * 16 + 12, r * 128 : (r + 1) * 128] = w
-    share = jax.nn.sigmoid(dot_nt(h3[...], wideh[...]))
+        halo.wait_recv()
+
+    arrange(0, 2)
+    inside = 1.0 - lacks.astype(F32)
+    conv1(1)
+    conv1(0, (inside, inside))
+    conv2(1)
+    conv2(0, (inside, 1.0))
+    conv3(1)
+    conv3(0)
+
+    share = jax.nn.sigmoid(
+        dot_nt(jnp.concatenate([h3[q] for q in range(4)], axis=1), wideh[...])
+    )
     sums = [jnp.zeros((SUB, 128), F32), jnp.zeros((SUB, 128), F32)]
     for j in range(STEP):
         v = share[j * SUB : (j + 1) * SUB]
@@ -291,7 +299,7 @@
         pair = []
         for s, ids in zip(sums, (ids1, ids2)):
             v = jnp.sum(s[4 * g : 4 * g + 4], axis=0, keepdims=True)
-            v = jnp.where(lane8 // 16 == sub8, jnp.broadcast_to(v, (HALF, 128)), 0.0)
+            v = jnp.where(mine8, jnp.broadcast_to(v, (HALF, 128)), 0.0)
             for shift in (64, 32, 16):
                 v = v + pltpu.roll(v, shift, axis=1)
             pair.append(jnp.where(lane8 % 16 == 12, jnp.broadcast_to(ids[g], (HALF, 128)), v))
@@ -308,7 +316,7 @@
     routed = dot_tn(to_owner.astype(BF16), parts.astype(BF16))[:NT]
     sendb[...] = routed.reshape(NT, 1, 128)
 
-    pl.semaphore_wait(c_sem, 1)
+    pl.semaphore_wait(y_sem, 7)
     me = chan * NT + tile
     recvb[me] = sendb[tile]
     mine_at = greet_order(tile) * 2 + chan
@@ -341,7 +349,11 @@
     bucket(total, cells[...], precip, temp, pet, out)
 
     pltpu.make_async_copy(recvb.at[rest], recvb.at[rest], row_send).wait()
-    halo.wait_send()
+
+    @pl.when(gives)
+    def _():
+        halo.wait_send()
+
     for copy in weights:
         copy.wait_send()
 
@@ -424,7 +436,7 @@
         + theirs
         + [
             pltpu.VMEM((4, 48 * TH, 128), F32),
-            pltpu.VMEM((22 * CP, W), BF16),
+            pltpu.VMEM((19 * CP, W), BF16),
             pltpu.VMEM((W, W), BF16),
             pltpu.VMEM((768, 256), BF16),
             pltpu.VMEM((256, 1536), BF16),
@@ -433,7 +445,7 @@
             pltpu.VMEM((7, WP, 128), BF16),
             pltpu.VMEM((12, WP, 128), BF16),
             pltpu.VMEM((10, WP, 128), BF16),
-            pltpu.VMEM((W, 1024), BF16),
+            pltpu.VMEM((4, W, 256), BF16),
             pltpu.VMEM((NT, 1, 128), F32),
             pltpu.VMEM((2 * NT, 1, 128), F32),
             pltpu.SemaphoreType.DMA((10,)),
@@ -443,7 +455,6 @@
             pltpu.SemaphoreType.DMA((4,)),
             pltpu.SemaphoreType.DMA,
             pltpu.SemaphoreType.DMA,
-            pltpu.SemaphoreType.REGULAR,
             pltpu.SemaphoreType.REGULAR,
             pltpu.SemaphoreType.REGULAR,
         ],

time: 31.5 us -> 26.8 us (0.85)
  Pallas kernels: 29.8 us -> 25.1 us
    pallas_call x1, Pallas kernels: 29.8 us -> 25.1 us  [on_device(): pl.pallas_call(raster_kernel, out_shape=jax.ShapeDtypeStruct(precip.shape...]
where the time goes in v3:
time: 26.8 us; the launch traced here: 26.7 us
  Pallas kernels  25.1 us (94%)
  local copies, waits for them, and re-layouts  1.56 us (6%)
    pallas_call x1, Pallas kernels, on_device(): pl.pallas_call(raster_kernel, out_shape=jax.ShapeDtypeStruct(precip.shape...  25.1 us
    unnamed x1, local copies, waits for them, and re-layouts  1.56 us

profile of v3, /device:TPU:1, one launch (start us, length us, event | category | flops | bytes accessed | tf_op | source)
XLA Modules:
  0.0 26.7 jit_solution(3919414348501545548)
XLA Ops:
  0.0 25.1 %raster.1 = f32[30,8,128]{2,1,0:T(8,128)} custom-call(bf16[35,16,512]{2,1,0:T(8,128)(2,1)} %attr_in.1, s32[16,512]{1,0:T(8,128)} %cb_in.1, s32[1,128]{1,0:T(1,128)} %bitcast.9, bf16[3,3,35,64]{3,2,1,0:T(8,128)(2,1)} %bitcast.7, bf16[3,3,64,128]{3,2,1,0:T(8,128)(2,1)} %bitcast.5, bf16[3,3,64,128]{3,2,1,0:T(8,128)(2,1)} %bitcast.6, bf16[12,64]{1,0:T(8,128)(2,1)} %bitcast.8, ...), custom_call_target="tpu_custom_call" | custom-call | tf_op jit(solution)/shard_map/raster/pallas_call | solution.py:430
  25.1 1.6 %copy.12 = f32[30,8,128]{2,1,0:T(8,128)} copy(f32[30,8,128]{2,1,0:T(8,128)} %raster.1) | data formatting | bytes 245760

commit v4 on v3

--- a/solution.py
+++ b/solution.py
@@ -17,6 +17,7 @@
 HALF = 8
 W = 512
 NT = 64
+GAP = TH + 1
 CP = 64
 SUB = 16
 STEP = W // SUB
@@ -68,12 +69,17 @@
     pl.semaphore_signal(sem, inc=1, device_id=where, device_id_type=MESH)
 
 
-def line_peers(tile):
-    lines = []
-    for weight in (1, 4, 16):
+LINES = (1, 4, 16)
+
+
+def signal_line(sem, tile, weights, way):
+    for weight in weights:
         at = lax.rem(tile // weight, 4)
-        lines.append([tile + (lax.rem(at + k, 4) - at) * weight for k in range(1, 4)])
-    return lines
+        for k in range(1, 4):
+
+            @pl.when(at + k < 4 if way > 0 else at >= k)
+            def _():
+                signal(sem, tile=tile + way * k * weight)
 
 
 def raster_kernel(
@@ -81,7 +87,7 @@
     attr, cb, cells, w1, w2, w3, hw, precip, temp, pet, w1r, w2r, w3r, hwr,
     spread, slots, perm, wide1, wide2, wide3, wideh, h0, h1, h2, h3, sendb, recvb,
     local_sems, halo_send, halo_recv, w_send, w_recv, row_send, row_recv,
-    z_sem, y_sem,
+    line_sem, z_sem, y_sem,
 ):
     tile = lax.axis_index("tile")
     chan = lax.axis_index("chan")
@@ -107,20 +113,23 @@
     towards = jnp.where(gives, tile + step, tile - step)
     source = jnp.where(lacks, tile + step, tile - step)
     signal(barrier, chan=1 - chan)
-    x_peers, z_peers, y_peers = line_peers(tile)
+    coords = [lax.rem(tile // weight, 4) for weight in LINES]
+    earlier = coords[0] + coords[1] + coords[2]
+    late_half = coords[2] // 2
 
     @pl.when(jnp.logical_not(lacks))
     def _():
         signal(barrier, tile=source)
 
-    for peer in x_peers + z_peers + y_peers:
-        signal(barrier, tile=peer)
+    signal_line(barrier, tile, LINES, 1)
 
     place = lax.broadcasted_iota(jnp.int32, (W, W), 0)
     column = lax.broadcasted_iota(jnp.int32, (W, W), 1)
     perm[...] = ((place % SUB) * STEP + place // SUB == column).astype(F32).astype(BF16)
     wide1[...] = jnp.zeros(wide1.shape, BF16)
     wideh[...] = jnp.zeros(wideh.shape, BF16)
+    for g in range(4):
+        spread[g, A * GAP :, :] = jnp.zeros((48 * GAP - A * GAP, 128), F32)
     for wide in (wide2, wide3):
         wide[0:128, 1152:1536] = jnp.zeros((128, 384), BF16)
         wide[128:256, 0:384] = jnp.zeros((128, 384), BF16)
@@ -129,11 +138,18 @@
         for i in range(first, last):
             r = jnp.where(chan == 0, i, TH - 1 - i)
             for g in range(4):
-                part = spread[g, pl.ds(r, 48, stride=TH), :]
+                part = spread[g, pl.ds(r, 48, stride=GAP), :]
                 slots[(3 + i) * CP : (3 + i) * CP + 48, g * 128 : (g + 1) * 128] = part.astype(BF16)
             slots[(3 + i) * CP + 48 : (4 + i) * CP, :] = jnp.zeros((CP - 48, W), BF16)
 
-    pl.semaphore_wait(barrier, 10 + gives.astype(jnp.int32))
+    got_attr.wait()
+    for c in range(A):
+        field = attr[c].astype(F32)
+        for g in range(4):
+            spread[g, c * GAP : c * GAP + TH, :] = field[:, g * 128 : (g + 1) * 128]
+    place_rows(13, 16)
+
+    pl.semaphore_wait(barrier, 1 + earlier + gives.astype(jnp.int32))
     weights = [
         pltpu.make_async_remote_copy(
             src_ref=src,
@@ -147,31 +163,31 @@
     ]
     for copy in weights:
         copy.start()
-    for peer in z_peers:
-        signal(z_sem, tile=peer)
-
-    got_attr.wait()
-    flat = attr[...].reshape(A * TH, W)
-    for g in range(4):
-        spread[g, : A * TH, :] = flat[:, g * 128 : (g + 1) * 128].astype(F32)
-        spread[g, A * TH :, :] = jnp.zeros((48 * TH - A * TH, 128), F32)
-    place_rows(13, 16)
-    halo = pltpu.make_async_remote_copy(
-        src_ref=slots.at[pl.ds(16 * CP, 3 * CP)],
-        dst_ref=slots.at[pl.ds(0, 3 * CP)],
-        send_sem=halo_send,
-        recv_sem=halo_recv,
-        device_id={"tile": towards},
-        device_id_type=MESH,
-    )
+    halos = [
+        pltpu.make_async_remote_copy(
+            src_ref=slots.at[pl.ds((16 + k) * CP, 48)],
+            dst_ref=slots.at[pl.ds(k * CP, 48)],
+            send_sem=halo_send.at[k],
+            recv_sem=halo_recv.at[k],
+            device_id={"tile": towards},
+            device_id_type=MESH,
+        )
+        for k in range(3)
+    ]
 
     @pl.when(gives)
     def _():
-        halo.start()
+        for copy in halos:
+            copy.start()
+
+    signal_line(line_sem, tile, LINES, -1)
+    for k in range(3):
+        slots[k * CP + 48 : (k + 1) * CP, :] = jnp.zeros((CP - 48, W), BF16)
 
     @pl.when(lacks)
     def _():
-        slots[: 3 * CP, :] = jnp.zeros((3 * CP, W), BF16)
+        for k in range(3):
+            slots[k * CP : k * CP + 48, :] = jnp.zeros((48, W), BF16)
 
     place_rows(0, 11)
 
@@ -184,6 +200,14 @@
     arrange(2, 2)
     arrange(4, 2)
     arrange(6, 1)
+
+
+    @pl.when(earlier < 9)
+    def _():
+        pl.semaphore_wait(line_sem, 9 - earlier)
+
+    for k in range(1, 4):
+        signal(z_sem, tile=tile + (lax.rem(coords[1] + k, 4) - coords[1]) * 4)
 
     sub8 = lax.broadcasted_iota(jnp.int32, (HALF, 128), 0)
     lane8 = lax.broadcasted_iota(jnp.int32, (HALF, 128), 1)
@@ -265,16 +289,18 @@
     for pair in range(2, 5):
         conv2(pair)
     pl.semaphore_wait(z_sem, 3)
-    for peer in y_peers:
-        signal(y_sem, tile=peer)
-        signal(y_sem, tile=peer, chan=1 - chan)
-    signal(y_sem, chan=1 - chan)
+    for k in range(1, 4):
+        peer = tile + (lax.rem(coords[2] + k, 4) - coords[2]) * 16
+        signal(y_sem.at[late_half], tile=peer)
+        signal(y_sem.at[late_half], tile=peer, chan=1 - chan)
+    signal(y_sem.at[late_half], chan=1 - chan)
     for pair in range(2, 4):
         conv3(pair)
 
     @pl.when(jnp.logical_not(lacks))
     def _():
-        halo.wait_recv()
+        for copy in halos:
+            copy.wait_recv()
 
     arrange(0, 2)
     inside = 1.0 - lacks.astype(F32)
@@ -316,21 +342,32 @@
     routed = dot_tn(to_owner.astype(BF16), parts.astype(BF16))[:NT]
     sendb[...] = routed.reshape(NT, 1, 128)
 
-    pl.semaphore_wait(y_sem, 7)
     me = chan * NT + tile
     recvb[me] = sendb[tile]
     mine_at = greet_order(tile) * 2 + chan
-    for i in range(2 * NT - 1):
-        swap = mine_at == i
-        o = jnp.where(swap, NT - 1, greet_tile(i // 2))
+
+    def send_row(o, c):
         pltpu.make_async_remote_copy(
             src_ref=sendb.at[o],
             dst_ref=recvb.at[me],
             send_sem=row_send,
             recv_sem=row_recv,
-            device_id={"tile": o, "chan": jnp.where(swap, 1, i % 2)},
+            device_id={"tile": o, "chan": c},
             device_id_type=MESH,
         ).start()
+
+    for half in range(2):
+        pl.semaphore_wait(y_sem.at[half], jnp.where(late_half == half, 3, 4))
+        last = (half + 1) * NT - 1
+        for i in range(half * NT, last):
+            swap = mine_at == i
+            o = jnp.where(swap, greet_tile(last // 2), greet_tile(i // 2))
+            send_row(o, jnp.where(swap, last % 2, i % 2))
+
+        @pl.when(late_half != half)
+        def _():
+            send_row(greet_tile(last // 2), last % 2)
+
     rest = pl.ds(0, 2 * NT - 1)
     pltpu.make_async_copy(recvb.at[rest], recvb.at[rest], row_recv).wait()
     got = recvb[...].reshape(2, NT, 128)
@@ -352,7 +389,8 @@
 
     @pl.when(gives)
     def _():
-        halo.wait_send()
+        for copy in halos:
+            copy.wait_send()
 
     for copy in weights:
         copy.wait_send()
@@ -435,7 +473,7 @@
         scratch_shapes=held
         + theirs
         + [
-            pltpu.VMEM((4, 48 * TH, 128), F32),
+            pltpu.VMEM((4, 48 * GAP, 128), F32),
             pltpu.VMEM((19 * CP, W), BF16),
             pltpu.VMEM((W, W), BF16),
             pltpu.VMEM((768, 256), BF16),
@@ -449,14 +487,15 @@
             pltpu.VMEM((NT, 1, 128), F32),
             pltpu.VMEM((2 * NT, 1, 128), F32),
             pltpu.SemaphoreType.DMA((10,)),
-            pltpu.SemaphoreType.DMA,
-            pltpu.SemaphoreType.DMA,
+            pltpu.SemaphoreType.DMA((3,)),
+            pltpu.SemaphoreType.DMA((3,)),
             pltpu.SemaphoreType.DMA((4,)),
             pltpu.SemaphoreType.DMA((4,)),
             pltpu.SemaphoreType.DMA,
             pltpu.SemaphoreType.DMA,
             pltpu.SemaphoreType.REGULAR,
             pltpu.SemaphoreType.REGULAR,
+            pltpu.SemaphoreType.REGULAR((2,)),
         ],
         compiler_params=pltpu.CompilerParams(
             collective_id=0, has_side_effects=True, vmem_limit_bytes=56 * 1024 * 1024

time: 26.8 us -> 26.1 us (0.974)
  Pallas kernels: 25.1 us -> 24.3 us
    pallas_call x1, Pallas kernels: 25.1 us -> 24.3 us  [on_device(): pl.pallas_call(raster_kernel, out_shape=jax.ShapeDtypeStruct(precip.shape...]
where the time goes in v4:
time: 26.1 us; the launch traced here: 25.9 us
  Pallas kernels  24.3 us (93%)
  local copies, waits for them, and re-layouts  1.56 us (6%)
    pallas_call x1, Pallas kernels, on_device(): pl.pallas_call(raster_kernel, out_shape=jax.ShapeDtypeStruct(precip.shape...  24.3 us
    unnamed x1, local copies, waits for them, and re-layouts  1.56 us

profile of v4, /device:TPU:1, one launch (start us, length us, event | category | flops | bytes accessed | tf_op | source)
XLA Modules:
  0.0 25.9 jit_solution(12245596457531151163)
XLA Ops:
  0.0 24.3 %raster.1 = f32[30,8,128]{2,1,0:T(8,128)} custom-call(bf16[35,16,512]{2,1,0:T(8,128)(2,1)} %attr_in.1, s32[16,512]{1,0:T(8,128)} %cb_in.1, s32[1,128]{1,0:T(1,128)} %bitcast.9, bf16[3,3,35,64]{3,2,1,0:T(8,128)(2,1)} %bitcast.7, bf16[3,3,64,128]{3,2,1,0:T(8,128)(2,1)} %bitcast.5, bf16[3,3,64,128]{3,2,1,0:T(8,128)(2,1)} %bitcast.6, bf16[12,64]{1,0:T(8,128)(2,1)} %bitcast.8, ...), custom_call_target="tpu_custom_call" | custom-call | tf_op jit(solution)/shard_map/raster/pallas_call | solution.py:468
  24.4 1.6 %copy.12 = f32[30,8,128]{2,1,0:T(8,128)} copy(f32[30,8,128]{2,1,0:T(8,128)} %raster.1) | data formatting | bytes 245760

commit v5 on v4

--- a/solution.py
+++ b/solution.py
@@ -414,8 +414,9 @@
     dry = lp * fc
     per_dry = 1.0 / dry
     per_fc = 1.0 / fc
+    power = beta * 1.4426950408889634
     snow = jnp.zeros(shape, F32)
-    soil = 0.5 * fc
+    soil = jnp.full(shape, 0.5, F32)
     upper = jnp.full(shape, 5.0, F32)
     lower = jnp.full(shape, 20.0, F32)
     runoff = []
@@ -427,11 +428,13 @@
         gained = snow + (rain - wet)
         snow = jnp.maximum(gained - cfmax * jnp.maximum(warm, 0.0), 0.0)
         inflow = wet + (gained - snow)
-        recharge = inflow * jnp.exp(beta * jnp.log(soil * per_fc))
-        soil = soil + inflow - recharge
-        excess = jnp.maximum(soil - fc, 0.0)
-        soil = soil - excess
-        soil = jnp.where(soil < dry, soil * (1.0 - demand * per_dry), soil - demand)
+        share = jnp.exp2(power * jnp.log(soil))
+        recharge = inflow * share
+        filled = soil + inflow * per_fc
+        filled = filled - (inflow * per_fc) * share
+        excess = jnp.maximum(filled - 1.0, 0.0) * fc
+        soil = jnp.minimum(filled, 1.0)
+        soil = jnp.where(soil < lp, soil * (1.0 - demand * per_dry), soil - demand * per_fc)
         upper = upper + recharge + excess
         upper_new = jnp.maximum(upper - perc, 0.0)
         lower = lower + upper - upper_new
@@ -467,7 +470,7 @@
     theirs = [pltpu.VMEM(args[k].shape, BF16) for k in (3, 4, 5, 6)]
     return pl.pallas_call(
         raster_kernel,
-        out_shape=jax.ShapeDtypeStruct(precip.shape, F32),
+        out_shape=pltpu.VMEM(precip.shape, F32),
         in_specs=[pl.BlockSpec(memory_space=pltpu.HBM)] * len(args),
         out_specs=pl.BlockSpec(memory_space=pltpu.VMEM),
         scratch_shapes=held

time: 26.1 us -> 24.4 us (0.935)
  local copies, waits for them, and re-layouts: 1.56 us -> 0.65 us
  Pallas kernels: 24.3 us -> 23.6 us
    unnamed x1, local copies, waits for them, and re-layouts: 1.56 us -> 0.65 us
    pallas_call x1, Pallas kernels: 24.3 us -> 23.6 us  [on_device(): pl.pallas_call(raster_kernel, out_shape=pltpu.VMEM(precip.shape, F32), in...]
where the time goes in v5:
time: 24.4 us; the launch traced here: 24.2 us
  Pallas kernels  23.6 us (97%)
  local copies, waits for them, and re-layouts  0.65 us (3%)
    pallas_call x1, Pallas kernels, on_device(): pl.pallas_call(raster_kernel, out_shape=pltpu.VMEM(precip.shape, F32), in...  23.6 us
    unnamed x1, local copies, waits for them, and re-layouts  0.65 us

profile of v5, /device:TPU:1, one launch (start us, length us, event | category | flops | bytes accessed | tf_op | source)
XLA Modules:
  0.0 24.2 jit_solution(15612415349760665877)
XLA Ops:
  0.0 23.6 %raster.1 = f32[30,8,128]{2,1,0:T(8,128)S(1)} custom-call(bf16[35,16,512]{2,1,0:T(8,128)(2,1)} %attr_in.1, s32[16,512]{1,0:T(8,128)} %cb_in.1, s32[1,128]{1,0:T(1,128)} %bitcast.9, bf16[3,3,35,64]{3,2,1,0:T(8,128)(2,1)} %bitcast.7, bf16[3,3,64,128]{3,2,1,0:T(8,128)(2,1)} %bitcast.5, bf16[3,3,64,128]{3,2,1,0:T(8,128)(2,1)} %bitcast.6, ...), custom_call_target="tpu_custom_call" | custom-call | tf_op jit(solution)/shard_map/raster/pallas_call | solution.py:471
  23.6 0.7 %copy.12 = f32[30,8,128]{2,1,0:T(8,128)} copy(f32[30,8,128]{2,1,0:T(8,128)S(1)} %raster.1) | data formatting | bytes 245760
